TPU v7x, 32 devices: a whole 2x2x4 slice. The times are simulated.
32 devices in a mesh: freq: 4 (over z), src: 8 (over y, x, core).
Axes of the slice: x: 2, y: 2, z: 4, core: 2. Of those that a mesh axis runs over, the one named last changes fastest.
Arguments:
- reflection: bfloat16 [2, 64, 1024, 1024], P(None, 'freq', None, 'src'), may hold values from -0.1875 to 0.1875
- direct_wave: float32 [1024, 64, 128], P('src', 'freq'), may hold values from -6 to 6
- first_arrival: int32 [1024, 64], P(('src', 'freq')), may hold values from 64 to 191
Outputs:
- focus_minus: float32 [1024, 64, 128], P('src', 'freq')
- focus_plus: float32 [1024, 64, 128], P('src', 'freq')
All inputs are finite; a program needn't handle non-finite values.
Results may differ from a plain program's by a relative error of at most 0.035.
Values may be sent and summed in bfloat16 or wider, within the bound.
No kernel may reach another device: no remote copies, remote signals or barrier semaphores. Data moves between devices by JAX's collectives and lax.ppermute only.
A program may use at most 128 MiB of HBM per device.

v0:
```python
import math

import jax
import jax.numpy as jnp
from jax import lax
from jax.sharding import PartitionSpec as P

NT = 512
ITERS = 2


def transform_tables(nfreq, ntime):
    freqs = jnp.arange(1, nfreq + 1, dtype=jnp.int32)
    times = jnp.arange(ntime, dtype=jnp.int32)
    phase = (freqs[:, None] * times[None, :] % ntime).astype(jnp.float32) * (2.0 * math.pi / ntime)
    cosine = jnp.cos(phase)
    sine = jnp.sin(phase)
    inverse = jnp.stack([cosine * (2.0 / ntime), -sine * (2.0 / ntime)]).astype(jnp.bfloat16)
    forward = jnp.stack([cosine, -sine]).astype(jnp.bfloat16)
    return (inverse, forward)


def apply_window(spectrum, first_arrival, inverse, forward):
    rows_count, nfreq, width = spectrum.shape
    half = width // 2
    ntime = inverse.shape[2]
    split = spectrum.reshape(rows_count, nfreq, 2, half)
    signal = jnp.einsum("rfpc,pft->rct", split, inverse, preferred_element_type=jnp.float32)
    times = jnp.arange(ntime, dtype=jnp.int32)
    limit = first_arrival[:, :, None]
    keep = (times[None, None, :] < limit) | (times[None, None, :] > ntime - limit)
    windowed = jnp.where(keep, signal, jnp.zeros_like(signal)).astype(jnp.bfloat16)
    back = jnp.einsum("rct,pft->rfpc", windowed, forward, preferred_element_type=jnp.float32)
    return back.reshape(rows_count, nfreq, width)


def stacked_parts(vectors, factor):
    rounded = vectors.astype(jnp.bfloat16)
    half = rounded.shape[-1] // 2
    swapped = jnp.concatenate([-rounded[..., half:], rounded[..., :half]], axis=-1)
    if factor < 0:
        swapped = -swapped
    return jnp.stack([rounded, swapped])


def to_owners(reflection, vectors, factor):
    operand = stacked_parts(vectors, factor)
    summed = lax.psum_scatter(
        jnp.einsum(
            "pfrs,psfk->rfk", reflection, operand, preferred_element_type=jnp.float32
        ).astype(jnp.bfloat16),
        "src",
        scatter_dimension=0,
        tiled=True,
    )
    return lax.all_to_all(summed, "freq", split_axis=0, concat_axis=1, tiled=True)


def to_groups(spectrum):
    return lax.all_to_all(
        spectrum.astype(jnp.bfloat16), "freq", split_axis=1, concat_axis=0, tiled=True
    ).astype(spectrum.dtype)


def local(reflection, direct_wave, first_arrival):
    nfreq = direct_wave.shape[1] * lax.axis_size("freq")
    inverse, forward = transform_tables(nfreq, NT)
    focus_plus = direct_wave
    focus_minus = direct_wave
    for iteration in range(ITERS):
        spectrum = to_owners(reflection, focus_plus, 1.0)
        focus_minus = to_groups(apply_window(spectrum, first_arrival, inverse, forward))
        spectrum = to_owners(reflection, focus_minus, -1.0)
        update = to_groups(apply_window(spectrum, first_arrival, inverse, forward))
        focus_plus = direct_wave + update
    return (focus_minus, focus_plus)


def solution(mesh):
    in_specs = (P(None, "freq", None, "src"), P("src", "freq", None), P(("src", "freq"), None))
    out_specs = (P("src", "freq", None), P("src", "freq", None))
    return jax.shard_map(local, mesh=mesh, in_specs=in_specs, out_specs=out_specs, check_vma=False)
```

profile of v0, /device:TPU:0, one launch (start us, length us, event | category | flops | bytes accessed | tf_op | source)
XLA Modules:
  0.0 458.8 jit_solution(8796098868735264194)
XLA Ops:
  7.2 1.6 copy.107
  9.1 8.2 %bitcast_convert_fusion.3 = bf16[16,128,1024]{2,1,0:T(8,128)(2,1)} fusion(bf16[2,16,1024,128]{3,2,1,0:T(8,128)(2,1)} %param.3, bf16[1,128,16,128]{1,3,0,2:T(8,128)(2,1)S(1)} %maximum_bitcast_fusion, bf16[1,128,16,128]{1,3,0,2:T(8,128)(2,1)S(1)} %convert_bitcast_fusion.2), kind=kOutput, calls=%fused_computation.3 | convolution fusion | flops 1076363264 | bytes 13631488 | tf_op jit(solution)/shard_map/pfrs,psfk->rfk/dot_general | solution.py:49
  17.3 6.5 %copy.155 = bf16[1024,2048]{1,0:T(8,128)(2,1)} copy(bf16[1024,2048]{0,1:T(8,128)(2,1)} %bitcast.209) | data formatting | bytes 8388608
  23.8 54.2 %reduce-scatter.13.cloned.1.call-done = bf16[128,2048]{1,0:T(8,128)(2,1)} async-done(((bf16[1024,2048]{1,0:T(8,128)(2,1)}), bf16[128,2048]{1,0:T(8,128)(2,1)}) %reduce-scatter.13.cloned.1.call-update) | async-done | bytes 524304
  78.0 1.3 copy.156
  80.5 4.6 %all-to-all-start = ((bf16[128,16,128]{2,1,0:T(8,128)(2,1)}), bf16[128,16,128]{2,1,0:T(8,128)(2,1)S(1)}, u32[]{:S(2)}, u32[]{:S(2)}) async-start(bf16[128,16,128]{2,1,0:T(8,128)(2,1)} %copy.88), calls=%async_computation | async-start | bytes 1048576 | tf_op jit(solution)/shard_map/all_to_all | solution.py:56
  85.7 13.8 %all-to-all-done = bf16[128,16,128]{2,1,0:T(8,128)(2,1)S(1)} async-done(((bf16[128,16,128]{2,1,0:T(8,128)(2,1)}), bf16[128,16,128]{2,1,0:T(8,128)(2,1)S(1)}, u32[]{:S(2)}, u32[]{:S(2)}) %all-to-all-start) | async-done | bytes 524320 | tf_op jit(solution)/shard_map/all_to_all | solution.py:56
  100.1 3.2 fusion.50
  103.3 2.3 copy.139
  106.1 16.4 %all_to_all.114 = bf16[32,64,128]{2,0,1:T(8,128)(2,1)S(1)} all-to-all(bf16[32,64,128]{2,0,1:T(8,128)(2,1)S(1)} %reshape.277), channel_id=1, replica_groups=mesh['freq'=4,'src'=8] {'freq'}, dimensions={1} | all-to-all | bytes 1048576 | tf_op jit(solution)/shard_map/all_to_all | solution.py:60
  124.5 8.2 %bitcast_convert_fusion.2 = bf16[16,128,1024]{2,1,0:T(8,128)(2,1)} fusion(bf16[2,16,1024,128]{3,2,1,0:T(8,128)(2,1)} %param.3, bf16[1,128,16,128]{1,3,0,2:T(8,128)(2,1)S(1)} %maximum_negate_fusion, bf16[1,128,16,128]{1,3,0,2:T(8,128)(2,1)S(1)} %copy.98), kind=kOutput, calls=%fused_computation.2 | convolution fusion | flops 1076363264 | bytes 13631488 | tf_op jit(solution)/shard_map/pfrs,psfk->rfk/dot_general | solution.py:49
  132.7 6.5 %copy.158 = bf16[1024,2048]{1,0:T(8,128)(2,1)} copy(bf16[1024,2048]{0,1:T(8,128)(2,1)} %bitcast.210) | data formatting | bytes 8388608
  139.2 49.6 %reduce-scatter.15.cloned.1.call-done = bf16[128,2048]{1,0:T(8,128)(2,1)} async-done(((bf16[1024,2048]{1,0:T(8,128)(2,1)}), bf16[128,2048]{1,0:T(8,128)(2,1)}) %reduce-scatter.15.cloned.1.call-update) | async-done | bytes 524304
  188.8 1.3 copy.159
  190.6 18.9 %all_to_all.115 = bf16[128,16,128]{2,1,0:T(8,128)(2,1)S(1)} all-to-all(bf16[128,16,128]{2,1,0:T(8,128)(2,1)S(1)} %copy.100), channel_id=1, replica_groups=mesh['freq'=4,'src'=8] {'freq'}, dimensions={0} | all-to-all | bytes 1048576 | tf_op jit(solution)/shard_map/all_to_all | solution.py:56
  209.9 3.2 fusion.47
  213.1 2.3 copy.142
  215.9 16.5 %all_to_all.116 = bf16[32,64,128]{2,0,1:T(8,128)(2,1)S(1)} all-to-all(bf16[32,64,128]{2,0,1:T(8,128)(2,1)S(1)} %reshape.278), channel_id=1, replica_groups=mesh['freq'=4,'src'=8] {'freq'}, dimensions={1} | all-to-all | bytes 1048576 | tf_op jit(solution)/shard_map/all_to_all | solution.py:60
  233.6 8.2 %bitcast_convert_fusion.1 = bf16[16,128,1024]{2,1,0:T(8,128)(2,1)} fusion(bf16[2,16,1024,128]{3,2,1,0:T(8,128)(2,1)} %param.3, bf16[1,128,16,128]{1,3,0,2:T(8,128)(2,1)S(1)} %maximum_bitcast_fusion.1, bf16[1,128,16,128]{1,3,0,2:T(8,128)(2,1)S(1)} %bitcast.217), kind=kOutput, calls=%fused_computation.1 | convolution fusion | flops 1076363264 | bytes 13631488 | tf_op jit(solution)/shard_map/pfrs,psfk->rfk/dot_general | solution.py:49
  241.7 6.5 %copy.161 = bf16[1024,2048]{1,0:T(8,128)(2,1)} copy(bf16[1024,2048]{0,1:T(8,128)(2,1)} %bitcast.211) | data formatting | bytes 8388608
  248.5 49.3 %reduce-scatter.17.cloned.1.call-done = bf16[128,2048]{1,0:T(8,128)(2,1)} async-done(((bf16[1024,2048]{1,0:T(8,128)(2,1)}), bf16[128,2048]{1,0:T(8,128)(2,1)}) %reduce-scatter.17.cloned.1.call-update) | async-done | bytes 524304
  299.6 18.9 %all_to_all.117 = bf16[128,16,128]{2,1,0:T(8,128)(2,1)S(1)} all-to-all(bf16[128,16,128]{2,1,0:T(8,128)(2,1)S(1)} %copy.111), channel_id=1, replica_groups=mesh['freq'=4,'src'=8] {'freq'}, dimensions={0} | all-to-all | bytes 1048576 | tf_op jit(solution)/shard_map/all_to_all | solution.py:56
  319.0 2.2 fusion.44
  322.8 16.6 %all_to_all.118 = bf16[32,64,128]{2,0,1:T(8,128)(2,1)S(1)} all-to-all(bf16[32,64,128]{2,0,1:T(8,128)(2,1)S(1)} %reshape.279), channel_id=1, replica_groups=mesh['freq'=4,'src'=8] {'freq'}, dimensions={1} | all-to-all | bytes 1048576 | tf_op jit(solution)/shard_map/all_to_all | solution.py:60
  341.3 8.2 %bitcast_convert_fusion = bf16[16,128,1024]{2,1,0:T(8,128)(2,1)} fusion(bf16[2,16,1024,128]{3,2,1,0:T(8,128)(2,1)} %param.3, bf16[1,128,16,128]{1,3,0,2:T(8,128)(2,1)S(1)} %maximum_negate_fusion.1, bf16[1,128,16,128]{1,3,0,2:T(8,128)(2,1)S(1)} %copy.121), kind=kOutput, calls=%fused_computation | convolution fusion | flops 1076363264 | bytes 13631488 | tf_op jit(solution)/shard_map/pfrs,psfk->rfk/dot_general | solution.py:49
  349.5 6.5 %copy.164 = bf16[1024,2048]{1,0:T(8,128)(2,1)} copy(bf16[1024,2048]{0,1:T(8,128)(2,1)} %bitcast.212) | data formatting | bytes 8388608
  356.1 49.6 %reduce-scatter.19.cloned.1.call-done = bf16[128,2048]{1,0:T(8,128)(2,1)} async-done(((bf16[1024,2048]{1,0:T(8,128)(2,1)}), bf16[128,2048]{1,0:T(8,128)(2,1)}) %reduce-scatter.19.cloned.1.call-update) | async-done | bytes 524304
  407.4 18.9 %all_to_all.119 = bf16[128,16,128]{2,1,0:T(8,128)(2,1)S(1)} all-to-all(bf16[128,16,128]{2,1,0:T(8,128)(2,1)S(1)} %copy.123), channel_id=1, replica_groups=mesh['freq'=4,'src'=8] {'freq'}, dimensions={0} | all-to-all | bytes 1048576 | tf_op jit(solution)/shard_map/all_to_all | solution.py:56
  426.8 3.2 fusion.41
  430.0 2.3 copy.146
  433.6 3.5 all-to-all-start.7
  438.2 12.5 %all-to-all-done.7 = bf16[32,64,128]{2,0,1:T(8,128)(2,1)S(1)} async-done(((bf16[32,64,128]{2,0,1:T(8,128)(2,1)}), bf16[32,64,128]{2,0,1:T(8,128)(2,1)S(1)}, u32[]{:S(2)}, u32[]{:S(2)}) %all-to-all-start.7) | async-done | bytes 524320 | tf_op jit(solution)/shard_map/all_to_all | solution.py:60
  (64 shorter events, 19.7 us)
Async XLA Ops:
  7.2 70.8 %reduce-scatter.13.cloned.1.call-start = ((), (), s32[]{:S(2)}) async-start(), calls=%async_computation.12 | async-start | bytes 4718592
  23.8 61.3 %copy-start.1 = (s32[32,64]{1,0:T(8,128)S(1)}, s32[32,64]{1,0:T(8,128)}, u32[]{:S(2)}) copy-start(s32[32,64]{1,0:T(8,128)} %param.5) | copy-start | bytes 24580
  80.5 19.1 %all-to-all-start = ((bf16[128,16,128]{2,1,0:T(8,128)(2,1)}), bf16[128,16,128]{2,1,0:T(8,128)(2,1)S(1)}, u32[]{:S(2)}, u32[]{:S(2)}) async-start(bf16[128,16,128]{2,1,0:T(8,128)(2,1)} %copy.88), calls=%async_computation | async-start | bytes 1048576 | tf_op jit(solution)/shard_map/all_to_all | solution.py:56
  85.1 103.7 %reduce-scatter.15.cloned.1.call-start = ((), (), s32[]{:S(2)}) async-start(), calls=%async_computation.13 | async-start | bytes 4718592
  139.2 158.7 %reduce-scatter.17.cloned.1.call-start = ((), (), s32[]{:S(2)}) async-start(), calls=%async_computation.14 | async-start | bytes 4718592
  248.3 157.4 %reduce-scatter.19.cloned.1.call-start = ((), (), s32[]{:S(2)}) async-start(), calls=%async_computation.15 | async-start | bytes 4718592
  432.3 18.8 %copy-start = (f32[128,16,128]{2,1,0:T(8,128)S(1)}, f32[128,16,128]{2,1,0:T(8,128)}, u32[]{:S(2)}) copy-start(f32[128,16,128]{2,1,0:T(8,128)} %param.4) | copy-start | bytes 3145732
  433.6 17.1 %all-to-all-start.7 = ((bf16[32,64,128]{2,0,1:T(8,128)(2,1)}), bf16[32,64,128]{2,0,1:T(8,128)(2,1)S(1)}, u32[]{:S(2)}, u32[]{:S(2)}) async-start(bf16[32,64,128]{2,0,1:T(8,128)(2,1)} %reshape.280), calls=%async_computation.7 | async-start | bytes 1048576 | tf_op jit(solution)/shard_map/all_to_all | solution.py:60
Sparse Core Ops, SparseCore 0:
  23.9 53.9 reduce-scatter.12
  139.3 49.4 reduce-scatter.14
  248.4 49.4 reduce-scatter.16
  356.2 49.4 reduce-scatter.18
where the time goes:
time: 460 us; the launch traced here: 459 us
  waiting for transfers between devices  229 us (50%)
  blocking collectives  106 us (23%)
  local copies, waits for them, and re-layouts  52.5 us (11%)
  matrix products  44.6 us (10%)
  between operations  14.1 us (3%)
  starting transfers between devices  8.42 us (2%)
    unnamed x8, waiting for transfers between devices  203 us
    all_to_all x3, blocking collectives, to_owners(): lax.all_to_all(summed, 'freq', split_axis=0, concat_axis=1, tiled=True)  56.7 us
    all_to_all x3, blocking collectives, to_groups(): lax.all_to_all(spectrum.astype(jnp.bfloat16), 'freq', split_axis=1, conca...  49.5 us
    unnamed x17, local copies, waits for them, and re-layouts  34.7 us
    dot_general x4, matrix products, to_owners(): jnp.einsum('pfrs,psfk->rfk', reflection, operand, preferred_element_type=...  32.7 us
    all_to_all x1, waiting for transfers between devices, to_owners(): lax.all_to_all(summed, 'freq', split_axis=0, concat_axis=1, tiled=True)  13.8 us
    all_to_all x1, waiting for transfers between devices, to_groups(): lax.all_to_all(spectrum.astype(jnp.bfloat16), 'freq', split_axis=1, conca...  12.5 us
    dot_general x4, matrix products, apply_window(): jnp.einsum('rct,pft->rfpc', windowed, forward, preferred_element_type=jnp...  11.9 us
  transfers between devices with their start and end apart: 6, of which 6 were waited for; matrix products, arithmetic and copies ran while one was open for 0% of the time, Pallas kernels for 0%

commit v1 on v0

v1 whole, which is shorter than its diff:
```python
import functools
import math

import jax
import jax.numpy as jnp
import ml_dtypes
import numpy as np
from jax import lax
from jax.experimental import pallas as pl
from jax.experimental.pallas import tpu as pltpu
from jax.sharding import PartitionSpec as P

NT = 512
ITERS = 2
KEPT = 192
CHUNKS = 2
MIB = 1 << 20
BF16, F32 = jnp.bfloat16, jnp.float32


def window_tables(nfreq, chunks, groups):
    freqs = np.arange(1, nfreq + 1)
    times = np.arange(KEPT)
    phase = ((freqs[:, None] * times[None, :]) % NT).astype(np.float32) * np.float32(2.0 * math.pi / NT)
    parts = np.stack([np.cos(phase), -np.sin(phase)])
    inverse = (parts * np.float32(2.0 / NT)).astype(ml_dtypes.bfloat16)
    forward = parts.astype(ml_dtypes.bfloat16).astype(np.float32) * np.where(times == 0, 1.0, 2.0)
    forward = forward.astype(ml_dtypes.bfloat16)

    def rows(table):
        table = table.reshape(2, groups, chunks, nfreq // groups // chunks, KEPT)
        return table.transpose(0, 2, 1, 3, 4).reshape(2 * nfreq, KEPT)

    return np.ascontiguousarray(rows(inverse).T), rows(forward)


def lane_index(shape):
    return lax.broadcasted_iota(jnp.int32, shape, len(shape) - 1)


def to_chunks(by_sub, lanes):
    n = len(by_sub)
    if n == 1:
        return by_sub
    width = 64 // n
    place = (lanes % 64) // width
    result = []
    for other in range(n):
        total = None
        for a in range(n):
            shift = ((a - other) * width) % 128
            moved = pltpu.roll(by_sub[a], shift, 1) if shift else by_sub[a]
            total = moved if total is None else jnp.where(place == a, moved, total)
        result.append(total)
    return result


def pack_kernel(chunks, f_dev, rows, dw_ref, *out_refs):
    fp = f_dev // chunks
    lanes = lane_index((rows, 128))
    for b in range(fp):
        values = [dw_ref[pl.ds(a * fp + b, rows, stride=f_dev), :] for a in range(chunks)]
        for chunk, value in enumerate(to_chunks(values, lanes)):
            out_refs[chunk][b] = value
            out_refs[chunks + chunk][b] = value.astype(BF16)


def unpack_kernel(chunks, f_dev, rows, has_wave, *refs):
    fp = f_dev // chunks
    lanes = lane_index((rows, 128))
    v_refs, out_ref = refs[:chunks], refs[-1]
    for b in range(fp):
        values = [v_refs[chunk][b].astype(F32) for chunk in range(chunks)]
        for a, value in enumerate(to_chunks(values, lanes)):
            place = pl.ds(a * fp + b, rows, stride=f_dev)
            if has_wave:
                value = value + refs[chunks][place, :]
            out_ref[place, :] = value


def assemble_kernel(n_f, has_wave, where_ref, *refs):
    blocks, out_ref = refs[:n_f], refs[-1]
    rows = blocks[0].shape[1]
    for k in range(n_f):
        place = pl.ds(pl.multiple_of((where_ref[0] ^ k) * rows, rows), rows)
        value = blocks[k][...]
        if has_wave:
            value = (refs[n_f][:, place, :] + value.astype(F32)).astype(BF16)
        out_ref[:, place, :] = value


def terms_kernel(chunks, n_chip, sign, order_ref, own_ref, other_ref, v_ref, w_ref, keep_ref, send_ref):
    lanes = lane_index(v_ref.shape[1:])
    place = (lanes % 64) // (64 // chunks)
    rows = []
    for ref in (v_ref, w_ref):
        value = ref[0].astype(F32)
        turned = pltpu.roll(value, 64, 1)
        turned = jnp.where((lanes < 64) == (sign > 0), -turned, turned)
        rows += [value, turned]
    weights = [
        jnp.concatenate([jnp.where(place == a, x, 0.0) for x in rows], axis=0).astype(BF16) for a in range(chunks)
    ]
    half = n_chip // 2
    for pos in range(n_chip):
        at = order_ref[pos]
        total = None
        for a in range(chunks):
            left = jnp.concatenate(
                [own_ref[0, a, 0, at, 0], own_ref[1, a, 0, at, 0], other_ref[0, a, 0, at], other_ref[1, a, 0, at]],
                axis=1,
            )
            part = jnp.dot(left, weights[a], preferred_element_type=F32)
            total = part if total is None else total + part
        if pos < half:
            keep_ref[pos, 0] = total.astype(BF16)
        else:
            send_ref[pos - half, 0] = total.astype(BF16)


def add_kernel(*refs):
    total = refs[0][...].astype(F32)
    for ref in refs[1:-1]:
        total = total + ref[...].astype(F32)
    refs[-1][...] = total.astype(BF16)


def split_kernel(n_in, n_f, where_ref, *refs):
    rows = refs[n_in].shape[1]
    for k in range(n_f):
        place = pl.ds(pl.multiple_of((where_ref[0] ^ k) * rows, rows), rows)
        total = refs[0][0, :, place, :].astype(F32)
        for ref in refs[1:n_in]:
            total = total + ref[0, :, place, :].astype(F32)
        refs[n_in + k][...] = total.astype(BF16)


def window_kernel(chunks, n_f, tile, where_ref, limit_ref, inv_ref, fwd_ref, *refs):
    blocks, outs, (gather, scatter) = refs[:n_f], refs[n_f : 2 * n_f], refs[2 * n_f :]
    fp, rows, _ = blocks[0].shape
    depth = n_f * fp
    for k in range(n_f):
        base = (where_ref[0] ^ k) * fp
        for b in range(fp):
            gather[pl.ds(base + b, rows, stride=depth), :] = blocks[k][b].astype(F32)
    lanes = lane_index((depth, 128))
    part, place = lanes // 64, (lanes % 64) // (64 // chunks)
    times = lax.broadcasted_iota(jnp.int32, (KEPT, 128), 0)
    width = 64 // chunks
    for first in range(0, rows, tile):
        columns = []
        for r in range(first, first + tile):
            value = gather[pl.ds(r * depth, depth), :]
            spread = []
            for a in range(chunks):
                total = value
                for other in range(chunks):
                    if other != a:
                        total = jnp.where(place == other, pltpu.roll(value, ((other - a) * width) % 128, 1), total)
                spread.append(total)
            stacked = [jnp.where(part == p, x, 0.0) for p in range(2) for x in spread]
            columns.append(jnp.concatenate(stacked, axis=0).astype(BF16))
        signal = jnp.dot(inv_ref[...], jnp.concatenate(columns, axis=1), preferred_element_type=F32)
        kept = []
        for i in range(tile):
            limit = limit_ref[pl.ds(first + i, 1), :]
            kept.append(jnp.where(times < limit, signal[:, i * 128 : (i + 1) * 128], 0.0).astype(BF16))
        back = jnp.dot(fwd_ref[...], jnp.concatenate(kept, axis=1), preferred_element_type=F32)
        for i in range(tile):
            total = None
            for p in range(2):
                for a in range(chunks):
                    at = (p * chunks + a) * depth
                    piece = back[at : at + depth, i * 128 : (i + 1) * 128]
                    total = piece if total is None else jnp.where((part == p) & (place == a), piece, total)
            scatter[pl.ds((first + i) * depth, depth), :] = total
    for k in range(n_f):
        base = (where_ref[0] ^ k) * fp
        for b in range(fp):
            outs[k][b] = scatter[pl.ds(base + b, rows, stride=depth), :].astype(BF16)


def vmem():
    return pl.BlockSpec(memory_space=pltpu.VMEM)


def smem():
    return pl.BlockSpec(memory_space=pltpu.SMEM)


def params(mib):
    return pltpu.CompilerParams(vmem_limit_bytes=mib * MIB)


def cost(flops, nbytes):
    return pl.CostEstimate(flops=int(flops), bytes_accessed=int(nbytes), transcendentals=0)


def bf16(*shape):
    return jax.ShapeDtypeStruct(shape, BF16)


class Plan:
    def __init__(self, reflection, direct_wave, first_arrival):
        self.n_f, self.n_s = lax.axis_size("freq"), lax.axis_size("src")
        self.q, self.f_dev, _ = direct_wave.shape
        self.chunks = CHUNKS
        self.fp = self.f_dev // self.chunks
        self.own_rows = self.q // self.n_f
        self.n_chip = self.n_s // 2
        self.bits = self.n_chip.bit_length() - 1
        z, s = lax.axis_index("freq"), lax.axis_index("src")
        chip, self.core = s // 2, s % 2
        self.where = z.reshape(1).astype(jnp.int32)
        orders = np.zeros((2, self.n_chip), np.int32)
        for core in range(2):
            for pos in range(self.n_chip):
                for stage in range(self.bits):
                    if pos >> (self.bits - 1 - stage) & 1:
                        orders[core, pos] ^= self.mask(stage, core)
        self.order = jnp.concatenate([chip ^ jnp.asarray(orders)[self.core], self.core[None]]).astype(jnp.int32)
        inverse, forward = window_tables(self.n_f * self.f_dev, self.chunks, self.n_f)
        self.inverse, self.forward = jnp.asarray(inverse), jnp.asarray(forward)
        split = first_arrival.reshape(self.own_rows, self.chunks, 1, 64 // self.chunks)
        split = jnp.broadcast_to(split, (self.own_rows, self.chunks, 2 * self.chunks, 64 // self.chunks))
        self.limits = [split[:, i].reshape(self.own_rows, 128) for i in range(self.chunks)]
        self.reflection = reflection.reshape(2, self.chunks, self.fp, self.n_chip, 2, self.q, self.q)
        send = lax.dynamic_index_in_dim(self.reflection, 1 - self.core, 4, keepdims=False)
        self.other = self.to_core(send)

    def mask(self, stage, core):
        return 1 << ((stage + core) % self.bits)

    def to_core(self, value):
        return lax.ppermute(value, "src", [(s, s ^ 1) for s in range(self.n_s)])

    def to_chip(self, value, stage):
        pairs = [(s, s ^ (self.mask(stage, s % 2) << 1)) for s in range(self.n_s)]
        return lax.ppermute(value, "src", pairs)

    def to_group(self, value, k):
        return lax.ppermute(value, "freq", [(z, z ^ k) for z in range(self.n_f)])

    def exchange(self, blocks):
        moved = {k: self.to_group(blocks[k], k) for k in range(self.n_f - 1, 0, -1)}
        return [blocks[0]] + [moved[k] for k in range(1, self.n_f)]

    def pack(self, direct_wave):
        whole = (self.fp, self.q, 128)
        out = pl.pallas_call(
            functools.partial(pack_kernel, self.chunks, self.f_dev, self.q),
            out_shape=[jax.ShapeDtypeStruct(whole, F32)] * self.chunks + [bf16(*whole)] * self.chunks,
            in_specs=[vmem()],
            out_specs=[vmem()] * (2 * self.chunks),
            compiler_params=params(16),
            name="pack",
        )(direct_wave.reshape(self.q * self.f_dev, 128))
        return out[: self.chunks], out[self.chunks :]

    def unpack(self, values, wave=None):
        waves = [] if wave is None else [wave.reshape(self.q * self.f_dev, 128)]
        out = pl.pallas_call(
            functools.partial(unpack_kernel, self.chunks, self.f_dev, self.q, wave is not None),
            out_shape=jax.ShapeDtypeStruct((self.q * self.f_dev, 128), F32),
            in_specs=[vmem()] * (self.chunks + len(waves)),
            out_specs=vmem(),
            compiler_params=params(16),
            name="unpack",
        )(*values, *waves)
        return out.reshape(self.q, self.f_dev, 128)

    def assemble(self, blocks, wave=None):
        waves = [] if wave is None else [wave]
        return pl.pallas_call(
            functools.partial(assemble_kernel, self.n_f, wave is not None),
            out_shape=bf16(self.fp, self.q, 128),
            in_specs=[smem()] + [vmem()] * (self.n_f + len(waves)),
            out_specs=vmem(),
            compiler_params=params(8),
            cost_estimate=cost(0, MIB // 2),
            name="assemble",
        )(self.where, *blocks, *waves)

    def terms(self, vector, other_vector, sign):
        half = self.n_chip // 2
        q, fp, chunks, n_chip = self.q, self.fp, self.chunks, self.n_chip
        out = bf16(half, fp, q, 128)
        out_spec = pl.BlockSpec((half, 1, q, 128), lambda b, order: (0, b, 0, 0))
        v_spec = pl.BlockSpec((1, q, 128), lambda b, order: (b, 0, 0))
        return pl.pallas_call(
            functools.partial(terms_kernel, chunks, n_chip, sign),
            out_shape=[out, out],
            grid_spec=pltpu.PrefetchScalarGridSpec(
                num_scalar_prefetch=1,
                grid=(fp,),
                in_specs=[
                    pl.BlockSpec(
                        (2, chunks, 1, n_chip, 1, q, q), lambda b, order: (0, 0, b, 0, order[n_chip], 0, 0)
                    ),
                    pl.BlockSpec((2, chunks, 1, n_chip, q, q), lambda b, order: (0, 0, b, 0, 0, 0)),
                    v_spec,
                    v_spec,
                ],
                out_specs=[out_spec, out_spec],
            ),
            compiler_params=params(16),
            cost_estimate=cost(4 * 2 * self.f_dev * n_chip * q * q * 128, 8 * MIB),
            name="terms",
        )(self.order, self.reflection, self.other, vector, other_vector)

    def add(self, values, half):
        spec = pl.BlockSpec((half, self.fp, self.q, 128), lambda i: (1, 0, 0, 0))
        return pl.pallas_call(
            add_kernel,
            out_shape=bf16(half, self.fp, self.q, 128),
            grid=(1,),
            in_specs=[spec] * len(values),
            out_specs=pl.BlockSpec((half, self.fp, self.q, 128), lambda i: (0, 0, 0, 0)),
            compiler_params=params(16),
            cost_estimate=cost(0, MIB),
            name="add",
        )(*values)

    def split(self, values):
        spec = pl.BlockSpec((1, self.fp, self.q, 128), lambda i: (0, 0, 0, 0))
        out = bf16(self.fp, self.own_rows, 128)
        out_spec = pl.BlockSpec(out.shape, lambda i: (0, 0, 0))
        return pl.pallas_call(
            functools.partial(split_kernel, len(values), self.n_f),
            out_shape=[out] * self.n_f,
            grid=(1,),
            in_specs=[smem()] + [spec] * len(values),
            out_specs=[out_spec] * self.n_f,
            compiler_params=params(16),
            cost_estimate=cost(0, MIB),
            name="split",
        )(self.where, *values)

    def window(self, blocks, chunk):
        out = bf16(self.fp, self.own_rows, 128)
        depth = self.n_f * self.fp
        scratch = pltpu.VMEM((self.own_rows * depth, 128), F32)
        return pl.pallas_call(
            functools.partial(window_kernel, self.chunks, self.n_f, min(4, self.own_rows)),
            out_shape=[out] * self.n_f,
            in_specs=[smem()] + [vmem()] * (3 + self.n_f),
            out_specs=[vmem()] * self.n_f,
            scratch_shapes=[scratch, scratch],
            compiler_params=params(16),
            cost_estimate=cost(2e9, MIB),
            name="window",
        )(self.where, self.limits[chunk], self.inverse, self.forward, *blocks)

    def theta(self, vector, chunk, sign):
        keep, send = self.terms(vector, self.to_core(vector), sign)
        addends, half = [keep], self.n_chip // 2
        for stage in range(self.bits):
            addends.append(self.to_chip(send, stage))
            half //= 2
            if half:
                send = self.add(addends, half)
        return self.exchange(self.window(self.exchange(self.split(addends)), chunk))


def local(reflection, direct_wave, first_arrival):
    plan = Plan(reflection, direct_wave, first_arrival)
    chunks = range(plan.chunks)
    waves, plus = plan.pack(direct_wave)
    for iteration in range(ITERS):
        minus = [plan.assemble(plan.theta(plus[i], i, 1)) for i in chunks]
        last = iteration == ITERS - 1
        plus = [plan.assemble(plan.theta(minus[i], i, -1), None if last else waves[i]) for i in chunks]
    return plan.unpack(minus), plan.unpack(plus, direct_wave)


def solution(mesh):
    in_specs = (P(None, "freq", None, "src"), P("src", "freq", None), P(("src", "freq"), None))
    out_specs = (P("src", "freq", None), P("src", "freq", None))
    return jax.shard_map(local, mesh=mesh, in_specs=in_specs, out_specs=out_specs, check_vma=False)
```

time: 460 us -> 281 us (0.61)
  waiting for transfers between devices: 229 us -> 81.9 us
  blocking collectives: 106 us -> 0 us
  Pallas kernels: 0 us -> 92.4 us
  starting transfers between devices: 8.42 us -> 87.6 us
  matrix products: 44.6 us -> 0 us
  local copies, waits for them, and re-layouts: 52.5 us -> 16.7 us
  between operations: 14.1 us -> 1.19 us
    unnamed x8 -> x0, waiting for transfers between devices: 203 us -> none
    all_to_all x6 -> x0, blocking collectives: 106 us -> none  [the longest x3 56.7 us: to_owners(): lax.all_to_all(summed, 'freq', split_axis=0, concat_axis=1, tiled=True)]
    pallas_call x0 -> x43, Pallas kernels: none -> 92.4 us  [the longest x8 62.2 us: terms(): pl.pallas_call(functools.partial(terms_kernel, chunks, n_chip, sign), out...]
    ppermute x0 -> x73, starting transfers between devices: none -> 87.6 us  [the longest x48 70.6 us: to_group(): return lax.ppermute(value, 'freq', [(z, z ^ k) for z in range(self.n_f)])]
    ppermute x0 -> x73, waiting for transfers between devices: none -> 81.9 us  [the longest x48 40.1 us: to_group(): return lax.ppermute(value, 'freq', [(z, z ^ k) for z in range(self.n_f)])]
    dot_general x8 -> x0, matrix products: 44.6 us -> none  [the longest x4 32.7 us: to_owners(): jnp.einsum('pfrs,psfk->rfk', reflection, operand, preferred_element_type=...]
    all_to_all x2 -> x0, waiting for transfers between devices: 26.4 us -> none  [the longest x1 13.8 us: to_owners(): lax.all_to_all(summed, 'freq', split_axis=0, concat_axis=1, tiled=True)]
    unnamed x17 -> x30, local copies, waits for them, and re-layouts: 34.7 us -> 10 us
  transfers between devices with their start and end apart: 6 -> 73, of which waited for: 6 -> 33; matrix products, arithmetic and copies ran while one was open for 0% -> 1% of each run, Pallas kernels for 0% -> 32%
where the time goes in v1:
time: 281 us; the launch traced here: 280 us
  Pallas kernels  92.4 us (33%)
  starting transfers between devices  87.6 us (31%)
  waiting for transfers between devices  81.9 us (29%)
  local copies, waits for them, and re-layouts  16.7 us (6%)
    ppermute x48, starting transfers between devices, to_group(): return lax.ppermute(value, 'freq', [(z, z ^ k) for z in range(self.n_f)])  70.6 us
    pallas_call x8, Pallas kernels, terms(): pl.pallas_call(functools.partial(terms_kernel, chunks, n_chip, sign), out...  62.2 us
    ppermute x48, waiting for transfers between devices, to_group(): return lax.ppermute(value, 'freq', [(z, z ^ k) for z in range(self.n_f)])  40.1 us
    ppermute x16, waiting for transfers between devices, to_chip(): return lax.ppermute(value, 'src', pairs)  37.4 us
    pallas_call x8, Pallas kernels, window(): pl.pallas_call(functools.partial(window_kernel, self.chunks, self.n_f, mi...  21.8 us
    ppermute x16, starting transfers between devices, to_chip(): return lax.ppermute(value, 'src', pairs)  15.6 us
    unnamed x30, local copies, waits for them, and re-layouts  10 us
  transfers between devices with their start and end apart: 73, of which 33 were waited for; matrix products, arithmetic and copies ran while one was open for 1% of the time, Pallas kernels for 32%

profile of v1, /device:TPU:0, one launch (start us, length us, event | category | flops | bytes accessed | tf_op | source)
XLA Modules:
  0.0 279.8 jit_solution(7403475249903015105)
XLA Ops:
  0.7 4.9 %dynamic-slice_bitcast_fusion = bf16[2,2,8,4,128,128]{5,4,3,2,1,0:T(8,128)(2,1)} fusion(bf16[2,2,8,4,2,128,128]{6,5,4,3,2,1,0:T(8,128)(2,1)} %bitcast.12, s32[]{:T(128)S(6)} %select_n.21), kind=kLoop, calls=%fused_computation | loop fusion | bytes 8388612 | tf_op jit(solution)/shard_map/jit(dynamic_index_in_dim)/squeeze | solution.py:228
  8.8 4.4 %collective-permute-done.28.w_ref = bf16[8,128,128]{2,1,0:T(8,128)(2,1)S(1)} collective-permute-done((bf16[8,128,128]{2,1,0:T(8,128)(2,1)S(1)}, bf16[8,128,128]{2,1,0:T(8,128)(2,1)S(1)}, u32[]{:S(2)}, u32[]{:S(2)}) %collective-permute-start.28) | collective-permute-done | bytes 262176 | tf_op jit(solution)/shard_map/ppermute | solution.py:235
  13.2 3.4 %copy-done = bf16[2,16,1024,128]{3,2,1,0:T(8,128)(2,1)S(1)} copy-done((bf16[2,16,1024,128]{3,2,1,0:T(8,128)(2,1)S(1)}, bf16[2,16,1024,128]{3,2,1,0:T(8,128)(2,1)}, u32[]{:S(2)}) %copy-start) | copy-done | bytes 8388632
  16.6 7.6 %terms.11 = (bf16[2,8,128,128]{3,2,1,0:T(8,128)(2,1)S(1)}, bf16[2,8,128,128]{3,2,1,0:T(8,128)(2,1)S(1)}) custom-call(s32[5]{0:T(128)S(1)} %pad_add_fusion.order_ref, bf16[2,2,8,4,2,128,128]{6,5,4,3,2,1,0:T(8,128)(2,1)S(1)} %bitcast.13, bf16[2,2,8,4,128,128]{5,4,3,2,1,0:T(8,128)(2,1)} %collective-permute-done.other_ref, ...), custom_call_target="tpu_custom_call" | custom-call | flops 1073741824 | bytes 8388608 | tf_op jit(solution)/shard_map/terms/pallas_call | solution.py:290
  24.3 2.9 %collective-permute-start.29 = (bf16[2,8,128,128]{3,2,1,0:T(8,128)(2,1)S(1)}, bf16[2,8,128,128]{3,2,1,0:T(8,128)(2,1)S(1)}, u32[]{:S(2)}, u32[]{:S(2)}) collective-permute-start(bf16[2,8,128,128]{3,2,1,0:T(8,128)(2,1)S(1)} %get-tuple-element.120), channel_id=1, source_target_pairs={{0,2},{1,5},{2,0},{3,7},{4,6},{5,1},{6,4},{7,3},{8,10},{9,13},{10,... | collective-permute-start | bytes 1572872 | tf_op jit(solution)/shard_map/ppermute | solution.py:239
  27.2 8.3 %terms.8 = (bf16[2,8,128,128]{3,2,1,0:T(8,128)(2,1)S(1)}, bf16[2,8,128,128]{3,2,1,0:T(8,128)(2,1)}) custom-call(s32[5]{0:T(128)S(1)} %pad_add_fusion.order_ref, bf16[2,2,8,4,2,128,128]{6,5,4,3,2,1,0:T(8,128)(2,1)S(1)} %bitcast.14, bf16[2,2,8,4,128,128]{5,4,3,2,1,0:T(8,128)(2,1)} %collective-permute-done.other_ref, ...), custom_call_target="tpu_custom_call" | custom-call | flops 1073741824 | bytes 8388608 | tf_op jit(solution)/shard_map/terms/pallas_call | solution.py:290
  39.0 8.4 %collective-permute-done.2.refs_1_ = bf16[2,8,128,128]{3,2,1,0:T(8,128)(2,1)S(1)} collective-permute-done((bf16[2,8,128,128]{3,2,1,0:T(8,128)(2,1)}, bf16[2,8,128,128]{3,2,1,0:T(8,128)(2,1)S(1)}, u32[]{:S(2)}, u32[]{:S(2)}) %collective-permute-start.2) | collective-permute-done | bytes 524320 | tf_op jit(solution)/shard_map/ppermute | solution.py:239
  56.9 3.0 %collective-permute-done.32.refs_2_ = bf16[8,32,128]{2,1,0:T(8,128)(2,1)S(1)} collective-permute-done((bf16[8,32,128]{2,1,0:T(8,128)(2,1)}, bf16[8,32,128]{2,1,0:T(8,128)(2,1)S(1)}, u32[]{:S(2)}, u32[]{:S(2)}) %collective-permute-start.32) | collective-permute-done | bytes 65568 | tf_op jit(solution)/shard_map/ppermute | solution.py:242
  63.4 2.7 window.11
  67.9 2.7 collective-permute-start.36
  79.1 2.7 window.8
  87.9 2.9 %collective-permute-done.9.refs_3_ = bf16[8,32,128]{2,1,0:T(8,128)(2,1)S(1)} collective-permute-done((bf16[8,32,128]{2,1,0:T(8,128)(2,1)S(1)}, bf16[8,32,128]{2,1,0:T(8,128)(2,1)S(1)}, u32[]{:S(2)}, u32[]{:S(2)}) %collective-permute-start.9) | collective-permute-done | bytes 65568 | tf_op jit(solution)/shard_map/ppermute | solution.py:242
  90.9 3.4 %copy-done.1 = bf16[2,16,1024,128]{3,2,1,0:T(8,128)(2,1)S(1)} copy-done((bf16[2,16,1024,128]{3,2,1,0:T(8,128)(2,1)S(1)}, bf16[2,16,1024,128]{3,2,1,0:T(8,128)(2,1)}, u32[]{:S(2)}) %copy-start.1) | copy-done | bytes 8388632
  94.3 7.6 %terms.12 = (bf16[2,8,128,128]{3,2,1,0:T(8,128)(2,1)S(1)}, bf16[2,8,128,128]{3,2,1,0:T(8,128)(2,1)S(1)}) custom-call(s32[5]{0:T(128)S(1)} %pad_add_fusion.order_ref, bf16[2,2,8,4,2,128,128]{6,5,4,3,2,1,0:T(8,128)(2,1)S(1)} %bitcast.15, bf16[2,2,8,4,128,128]{5,4,3,2,1,0:T(8,128)(2,1)} %collective-permute-done.other_ref, ...), custom_call_target="tpu_custom_call" | custom-call | flops 1073741824 | bytes 8388608 | tf_op jit(solution)/shard_map/terms/pallas_call | solution.py:290
  102.6 7.8 %terms.9 = (bf16[2,8,128,128]{3,2,1,0:T(8,128)(2,1)S(1)}, bf16[2,8,128,128]{3,2,1,0:T(8,128)(2,1)S(1)}) custom-call(s32[5]{0:T(128)S(1)} %pad_add_fusion.order_ref, bf16[2,2,8,4,2,128,128]{6,5,4,3,2,1,0:T(8,128)(2,1)S(1)} %bitcast.16, bf16[2,2,8,4,128,128]{5,4,3,2,1,0:T(8,128)(2,1)} %collective-permute-done.other_ref, ...), custom_call_target="tpu_custom_call" | custom-call | flops 1073741824 | bytes 8388608 | tf_op jit(solution)/shard_map/terms/pallas_call | solution.py:290
  112.4 8.9 %collective-permute-done.39.refs_2_ = bf16[1,8,128,128]{3,2,1,0:T(8,128)(2,1)S(1)} collective-permute-done((bf16[1,8,128,128]{3,2,1,0:T(8,128)(2,1)S(1)}, bf16[1,8,128,128]{3,2,1,0:T(8,128)(2,1)S(1)}, u32[]{:S(2)}, u32[]{:S(2)}) %collective-permute-start.39) | collective-permute-done | bytes 262176 | tf_op jit(solution)/shard_map/ppermute | solution.py:239
  129.7 2.7 window.12
  132.6 2.7 collective-permute-start.44
  146.0 2.7 window.9
  157.3 7.7 %terms.13 = (bf16[2,8,128,128]{3,2,1,0:T(8,128)(2,1)S(1)}, bf16[2,8,128,128]{3,2,1,0:T(8,128)(2,1)S(1)}) custom-call(s32[5]{0:T(128)S(1)} %pad_add_fusion.order_ref, bf16[2,2,8,4,2,128,128]{6,5,4,3,2,1,0:T(8,128)(2,1)S(1)} %bitcast.19, bf16[2,2,8,4,128,128]{5,4,3,2,1,0:T(8,128)(2,1)} %collective-permute-done.other_ref, ...), custom_call_target="tpu_custom_call" | custom-call | flops 1073741824 | bytes 8388608 | tf_op jit(solution)/shard_map/terms/pallas_call | solution.py:290
  165.6 7.6 %terms.10 = (bf16[2,8,128,128]{3,2,1,0:T(8,128)(2,1)S(1)}, bf16[2,8,128,128]{3,2,1,0:T(8,128)(2,1)S(1)}) custom-call(s32[5]{0:T(128)S(1)} %pad_add_fusion.order_ref, bf16[2,2,8,4,2,128,128]{6,5,4,3,2,1,0:T(8,128)(2,1)S(1)} %bitcast.20, bf16[2,2,8,4,128,128]{5,4,3,2,1,0:T(8,128)(2,1)} %collective-permute-done.other_ref, ...), custom_call_target="tpu_custom_call" | custom-call | flops 1073741824 | bytes 8388608 | tf_op jit(solution)/shard_map/terms/pallas_call | solution.py:290
  175.1 9.0 %collective-permute-done.48.refs_2_ = bf16[1,8,128,128]{3,2,1,0:T(8,128)(2,1)S(1)} collective-permute-done((bf16[1,8,128,128]{3,2,1,0:T(8,128)(2,1)S(1)}, bf16[1,8,128,128]{3,2,1,0:T(8,128)(2,1)S(1)}, u32[]{:S(2)}, u32[]{:S(2)}) %collective-permute-start.48) | collective-permute-done | bytes 262176 | tf_op jit(solution)/shard_map/ppermute | solution.py:239
  184.3 2.7 collective-permute-start.50
  189.9 3.2 %collective-permute-done.51.refs_3_ = bf16[8,32,128]{2,1,0:T(8,128)(2,1)S(1)} collective-permute-done((bf16[8,32,128]{2,1,0:T(8,128)(2,1)S(1)}, bf16[8,32,128]{2,1,0:T(8,128)(2,1)S(1)}, u32[]{:S(2)}, u32[]{:S(2)}) %collective-permute-start.51) | collective-permute-done | bytes 65568 | tf_op jit(solution)/shard_map/ppermute | solution.py:242
  193.1 2.7 window.13
  208.9 2.7 window.10
  217.5 2.9 %collective-permute-done.27.refs_3_ = bf16[8,32,128]{2,1,0:T(8,128)(2,1)S(1)} collective-permute-done((bf16[8,32,128]{2,1,0:T(8,128)(2,1)S(1)}, bf16[8,32,128]{2,1,0:T(8,128)(2,1)S(1)}, u32[]{:S(2)}, u32[]{:S(2)}) %collective-permute-start.27) | collective-permute-done | bytes 65568 | tf_op jit(solution)/shard_map/ppermute | solution.py:242
  220.5 7.9 %terms.15 = (bf16[2,8,128,128]{3,2,1,0:T(8,128)(2,1)S(1)}, bf16[2,8,128,128]{3,2,1,0:T(8,128)(2,1)S(1)}) custom-call(s32[5]{0:T(128)S(1)} %pad_add_fusion.order_ref, bf16[2,2,8,4,2,128,128]{6,5,4,3,2,1,0:T(8,128)(2,1)S(1)} %bitcast.21, bf16[2,2,8,4,128,128]{5,4,3,2,1,0:T(8,128)(2,1)} %collective-permute-done.other_ref, ...), custom_call_target="tpu_custom_call" | custom-call | flops 1073741824 | bytes 8388608 | tf_op jit(solution)/shard_map/terms/pallas_call | solution.py:290
  228.9 7.6 %terms.14 = (bf16[2,8,128,128]{3,2,1,0:T(8,128)(2,1)S(1)}, bf16[2,8,128,128]{3,2,1,0:T(8,128)(2,1)S(1)}) custom-call(s32[5]{0:T(128)S(1)} %pad_add_fusion.order_ref, bf16[2,2,8,4,2,128,128]{6,5,4,3,2,1,0:T(8,128)(2,1)S(1)} %bitcast.22, bf16[2,2,8,4,128,128]{5,4,3,2,1,0:T(8,128)(2,1)} %collective-permute-done.other_ref, ...), custom_call_target="tpu_custom_call" | custom-call | flops 1073741824 | bytes 8388608 | tf_op jit(solution)/shard_map/terms/pallas_call | solution.py:290
  238.7 9.9 %collective-permute-done.56.refs_1_ = bf16[2,8,128,128]{3,2,1,0:T(8,128)(2,1)S(1)} collective-permute-done((bf16[2,8,128,128]{3,2,1,0:T(8,128)(2,1)S(1)}, bf16[2,8,128,128]{3,2,1,0:T(8,128)(2,1)S(1)}, u32[]{:S(2)}, u32[]{:S(2)}) %collective-permute-start.56) | collective-permute-done | bytes 524320 | tf_op jit(solution)/shard_map/ppermute | solution.py:239
  259.7 2.7 window.15
  266.9 2.7 window.14
  (197 shorter events, 119.3 us)
Async XLA Ops:
  8.2 18.9 %collective-permute-start.1 = (bf16[8,128,128]{2,1,0:T(8,128)(2,1)S(1)}, bf16[8,128,128]{2,1,0:T(8,128)(2,1)S(1)}, u32[]{:S(2)}, u32[]{:S(2)}) collective-permute-start(bf16[8,128,128]{2,1,0:T(8,128)(2,1)S(1)} %get-tuple-element.86.v_ref), channel_id=1, source_target_pairs={{0,1},{1,0},{2,3},{3,2},{4,5},{5,4},{6,7},{7,6},{8,9},{9,8},{10,11... | collective-permute-start | bytes 786440 | tf_op jit(solution)/shard_map/ppermute | solution.py:235
  24.3 11.2 %collective-permute-start.29 = (bf16[2,8,128,128]{3,2,1,0:T(8,128)(2,1)S(1)}, bf16[2,8,128,128]{3,2,1,0:T(8,128)(2,1)S(1)}, u32[]{:S(2)}, u32[]{:S(2)}) collective-permute-start(bf16[2,8,128,128]{3,2,1,0:T(8,128)(2,1)S(1)} %get-tuple-element.120), channel_id=1, source_target_pairs={{0,2},{1,5},{2,0},{3,7},{4,6},{5,1},{6,4},{7,3},{8,10},{9,13},{10,... | collective-permute-start | bytes 1572872 | tf_op jit(solution)/shard_map/ppermute | solution.py:239
  35.5 11.9 %collective-permute-start.2 = (bf16[2,8,128,128]{3,2,1,0:T(8,128)(2,1)}, bf16[2,8,128,128]{3,2,1,0:T(8,128)(2,1)S(1)}, u32[]{:S(2)}, u32[]{:S(2)}) collective-permute-start(bf16[2,8,128,128]{3,2,1,0:T(8,128)(2,1)} %get-tuple-element.88), channel_id=1, source_target_pairs={{0,2},{1,5},{2,0},{3,7},{4,6},{5,1},{6,4},{7,3},{8,10},{9,13},{10,... | collective-permute-start | bytes 1572872 | tf_op jit(solution)/shard_map/ppermute | solution.py:239
  36.3 13.6 %collective-permute-start.30 = (bf16[1,8,128,128]{3,2,1,0:T(8,128)(2,1)}, bf16[1,8,128,128]{3,2,1,0:T(8,128)(2,1)}, u32[]{:S(2)}, u32[]{:S(2)}) collective-permute-start(bf16[1,8,128,128]{3,2,1,0:T(8,128)(2,1)} %add.29), channel_id=1, source_target_pairs={{0,4},{1,3},{2,6},{3,1},{4,0},{5,7},{6,2},{7,5},{8,12},{9,11},{10,... | collective-permute-start | bytes 786440 | tf_op jit(solution)/shard_map/ppermute | solution.py:239
  48.1 22.4 %collective-permute-start.3 = (bf16[1,8,128,128]{3,2,1,0:T(8,128)(2,1)}, bf16[1,8,128,128]{3,2,1,0:T(8,128)(2,1)S(1)}, u32[]{:S(2)}, u32[]{:S(2)}) collective-permute-start(bf16[1,8,128,128]{3,2,1,0:T(8,128)(2,1)} %add.26), channel_id=1, source_target_pairs={{0,4},{1,3},{2,6},{3,1},{4,0},{5,7},{6,2},{7,5},{8,12},{9,11},{10,... | collective-permute-start | bytes 786440 | tf_op jit(solution)/shard_map/ppermute | solution.py:239
  66.2 8.9 %collective-permute-start.35 = (bf16[8,32,128]{2,1,0:T(8,128)(2,1)S(1)}, bf16[8,32,128]{2,1,0:T(8,128)(2,1)S(1)}, u32[]{:S(2)}, u32[]{:S(2)}) collective-permute-start(bf16[8,32,128]{2,1,0:T(8,128)(2,1)S(1)} %get-tuple-element.127), channel_id=1, source_target_pairs={{0,16},{8,24},{16,0},{24,8},{1,17},{9,25},{17,1},{25,9},{2,18},{10... | collective-permute-start | bytes 196616 | tf_op jit(solution)/shard_map/ppermute | solution.py:242
  75.2 15.7 %collective-permute-start.37 = (bf16[8,128,128]{2,1,0:T(8,128)(2,1)S(1)}, bf16[8,128,128]{2,1,0:T(8,128)(2,1)S(1)}, u32[]{:S(2)}, u32[]{:S(2)}) collective-permute-start(bf16[8,128,128]{2,1,0:T(8,128)(2,1)S(1)} %assemble.11.v_ref), channel_id=1, source_target_pairs={{0,1},{1,0},{2,3},{3,2},{4,5},{5,4},{6,7},{7,6},{8,9},{9,8},{10,11... | collective-permute-start | bytes 786440 | tf_op jit(solution)/shard_map/ppermute | solution.py:235
  90.8 11.8 %collective-permute-start.10 = (bf16[8,128,128]{2,1,0:T(8,128)(2,1)S(1)}, bf16[8,128,128]{2,1,0:T(8,128)(2,1)S(1)}, u32[]{:S(2)}, u32[]{:S(2)}) collective-permute-start(bf16[8,128,128]{2,1,0:T(8,128)(2,1)S(1)} %assemble.8.v_ref), channel_id=1, source_target_pairs={{0,1},{1,0},{2,3},{3,2},{4,5},{5,4},{6,7},{7,6},{8,9},{9,8},{10,11... | collective-permute-start | bytes 786440 | tf_op jit(solution)/shard_map/ppermute | solution.py:235
  101.9 10.0 %collective-permute-start.38 = (bf16[2,8,128,128]{3,2,1,0:T(8,128)(2,1)S(1)}, bf16[2,8,128,128]{3,2,1,0:T(8,128)(2,1)S(1)}, u32[]{:S(2)}, u32[]{:S(2)}) collective-permute-start(bf16[2,8,128,128]{3,2,1,0:T(8,128)(2,1)S(1)} %get-tuple-element.130), channel_id=1, source_target_pairs={{0,2},{1,5},{2,0},{3,7},{4,6},{5,1},{6,4},{7,3},{8,10},{9,13},{10,... | collective-permute-start | bytes 1572872 | tf_op jit(solution)/shard_map/ppermute | solution.py:239
  110.4 15.4 %collective-permute-start.11 = (bf16[2,8,128,128]{3,2,1,0:T(8,128)(2,1)S(1)}, bf16[2,8,128,128]{3,2,1,0:T(8,128)(2,1)S(1)}, u32[]{:S(2)}, u32[]{:S(2)}) collective-permute-start(bf16[2,8,128,128]{3,2,1,0:T(8,128)(2,1)S(1)} %get-tuple-element.98), channel_id=1, source_target_pairs={{0,2},{1,5},{2,0},{3,7},{4,6},{5,1},{6,4},{7,3},{8,10},{9,13},{10,... | collective-permute-start | bytes 1572872 | tf_op jit(solution)/shard_map/ppermute | solution.py:239
  112.0 9.3 %collective-permute-start.39 = (bf16[1,8,128,128]{3,2,1,0:T(8,128)(2,1)S(1)}, bf16[1,8,128,128]{3,2,1,0:T(8,128)(2,1)S(1)}, u32[]{:S(2)}, u32[]{:S(2)}) collective-permute-start(bf16[1,8,128,128]{3,2,1,0:T(8,128)(2,1)S(1)} %add.30), channel_id=1, source_target_pairs={{0,4},{1,3},{2,6},{3,1},{4,0},{5,7},{6,2},{7,5},{8,12},{9,11},{10,... | collective-permute-start | bytes 786440 | tf_op jit(solution)/shard_map/ppermute | solution.py:239
  125.9 11.1 %collective-permute-start.12 = (bf16[1,8,128,128]{3,2,1,0:T(8,128)(2,1)S(1)}, bf16[1,8,128,128]{3,2,1,0:T(8,128)(2,1)S(1)}, u32[]{:S(2)}, u32[]{:S(2)}) collective-permute-start(bf16[1,8,128,128]{3,2,1,0:T(8,128)(2,1)S(1)} %add.27), channel_id=1, source_target_pairs={{0,4},{1,3},{2,6},{3,1},{4,0},{5,7},{6,2},{7,5},{8,12},{9,11},{10,... | collective-permute-start | bytes 786440 | tf_op jit(solution)/shard_map/ppermute | solution.py:239
  132.6 9.0 %collective-permute-start.44 = (bf16[8,32,128]{2,1,0:T(8,128)(2,1)S(1)}, bf16[8,32,128]{2,1,0:T(8,128)(2,1)S(1)}, u32[]{:S(2)}, u32[]{:S(2)}) collective-permute-start(bf16[8,32,128]{2,1,0:T(8,128)(2,1)S(1)} %get-tuple-element.137), channel_id=1, source_target_pairs={{0,16},{8,24},{16,0},{24,8},{1,17},{9,25},{17,1},{25,9},{2,18},{10... | collective-permute-start | bytes 196616 | tf_op jit(solution)/shard_map/ppermute | solution.py:242
  142.2 15.1 %collective-permute-start.46 = (bf16[8,128,128]{2,1,0:T(8,128)(2,1)S(1)}, bf16[8,128,128]{2,1,0:T(8,128)(2,1)S(1)}, u32[]{:S(2)}, u32[]{:S(2)}) collective-permute-start(bf16[8,128,128]{2,1,0:T(8,128)(2,1)S(1)} %assemble.12.v_ref), channel_id=1, source_target_pairs={{0,1},{1,0},{2,3},{3,2},{4,5},{5,4},{6,7},{7,6},{8,9},{9,8},{10,11... | collective-permute-start | bytes 786440 | tf_op jit(solution)/shard_map/ppermute | solution.py:235
  157.2 8.4 %collective-permute-start.19 = (bf16[8,128,128]{2,1,0:T(8,128)(2,1)S(1)}, bf16[8,128,128]{2,1,0:T(8,128)(2,1)S(1)}, u32[]{:S(2)}, u32[]{:S(2)}) collective-permute-start(bf16[8,128,128]{2,1,0:T(8,128)(2,1)S(1)} %assemble.9.v_ref), channel_id=1, source_target_pairs={{0,1},{1,0},{2,3},{3,2},{4,5},{5,4},{6,7},{7,6},{8,9},{9,8},{10,11... | collective-permute-start | bytes 786440 | tf_op jit(solution)/shard_map/ppermute | solution.py:235
  164.9 9.8 %collective-permute-start.47 = (bf16[2,8,128,128]{3,2,1,0:T(8,128)(2,1)S(1)}, bf16[2,8,128,128]{3,2,1,0:T(8,128)(2,1)S(1)}, u32[]{:S(2)}, u32[]{:S(2)}) collective-permute-start(bf16[2,8,128,128]{3,2,1,0:T(8,128)(2,1)S(1)} %get-tuple-element.141), channel_id=1, source_target_pairs={{0,2},{1,5},{2,0},{3,7},{4,6},{5,1},{6,4},{7,3},{8,10},{9,13},{10,... | collective-permute-start | bytes 1572872 | tf_op jit(solution)/shard_map/ppermute | solution.py:239
  173.2 15.5 %collective-permute-start.20 = (bf16[2,8,128,128]{3,2,1,0:T(8,128)(2,1)S(1)}, bf16[2,8,128,128]{3,2,1,0:T(8,128)(2,1)S(1)}, u32[]{:S(2)}, u32[]{:S(2)}) collective-permute-start(bf16[2,8,128,128]{3,2,1,0:T(8,128)(2,1)S(1)} %get-tuple-element.109), channel_id=1, source_target_pairs={{0,2},{1,5},{2,0},{3,7},{4,6},{5,1},{6,4},{7,3},{8,10},{9,13},{10,... | collective-permute-start | bytes 1572872 | tf_op jit(solution)/shard_map/ppermute | solution.py:239
  174.8 9.3 %collective-permute-start.48 = (bf16[1,8,128,128]{3,2,1,0:T(8,128)(2,1)S(1)}, bf16[1,8,128,128]{3,2,1,0:T(8,128)(2,1)S(1)}, u32[]{:S(2)}, u32[]{:S(2)}) collective-permute-start(bf16[1,8,128,128]{3,2,1,0:T(8,128)(2,1)S(1)} %add.31), channel_id=1, source_target_pairs={{0,4},{1,3},{2,6},{3,1},{4,0},{5,7},{6,2},{7,5},{8,12},{9,11},{10,... | collective-permute-start | bytes 786440 | tf_op jit(solution)/shard_map/ppermute | solution.py:239
  196.0 8.8 %collective-permute-start.53 = (bf16[8,32,128]{2,1,0:T(8,128)(2,1)S(1)}, bf16[8,32,128]{2,1,0:T(8,128)(2,1)S(1)}, u32[]{:S(2)}, u32[]{:S(2)}) collective-permute-start(bf16[8,32,128]{2,1,0:T(8,128)(2,1)S(1)} %get-tuple-element.148), channel_id=1, source_target_pairs={{0,16},{8,24},{16,0},{24,8},{1,17},{9,25},{17,1},{25,9},{2,18},{10... | collective-permute-start | bytes 196616 | tf_op jit(solution)/shard_map/ppermute | solution.py:242
  204.9 15.6 %collective-permute-start.64 = (bf16[8,128,128]{2,1,0:T(8,128)(2,1)S(1)}, bf16[8,128,128]{2,1,0:T(8,128)(2,1)S(1)}, u32[]{:S(2)}, u32[]{:S(2)}) collective-permute-start(bf16[8,128,128]{2,1,0:T(8,128)(2,1)S(1)} %assemble.13.refs_1_.v_ref), channel_id=1, source_target_pairs={{0,1},{1,0},{2,3},{3,2},{4,5},{5,4},{6,7},{7,6},{8,9},{9,8},{10,11... | collective-permute-start | bytes 786440 | tf_op jit(solution)/shard_map/ppermute | solution.py:235
  220.5 8.4 %collective-permute-start.55 = (bf16[8,128,128]{2,1,0:T(8,128)(2,1)S(1)}, bf16[8,128,128]{2,1,0:T(8,128)(2,1)S(1)}, u32[]{:S(2)}, u32[]{:S(2)}) collective-permute-start(bf16[8,128,128]{2,1,0:T(8,128)(2,1)S(1)} %assemble.10.refs_0_.v_ref), channel_id=1, source_target_pairs={{0,1},{1,0},{2,3},{3,2},{4,5},{5,4},{6,7},{7,6},{8,9},{9,8},{10,11... | collective-permute-start | bytes 786440 | tf_op jit(solution)/shard_map/ppermute | solution.py:235
  228.4 9.8 %collective-permute-start.65 = (bf16[2,8,128,128]{3,2,1,0:T(8,128)(2,1)S(1)}, bf16[2,8,128,128]{3,2,1,0:T(8,128)(2,1)S(1)}, u32[]{:S(2)}, u32[]{:S(2)}) collective-permute-start(bf16[2,8,128,128]{3,2,1,0:T(8,128)(2,1)S(1)} %get-tuple-element.161), channel_id=1, source_target_pairs={{0,2},{1,5},{2,0},{3,7},{4,6},{5,1},{6,4},{7,3},{8,10},{9,13},{10,... | collective-permute-start | bytes 1572872 | tf_op jit(solution)/shard_map/ppermute | solution.py:239
  236.5 12.1 %collective-permute-start.56 = (bf16[2,8,128,128]{3,2,1,0:T(8,128)(2,1)S(1)}, bf16[2,8,128,128]{3,2,1,0:T(8,128)(2,1)S(1)}, u32[]{:S(2)}, u32[]{:S(2)}) collective-permute-start(bf16[2,8,128,128]{3,2,1,0:T(8,128)(2,1)S(1)} %get-tuple-element.151), channel_id=1, source_target_pairs={{0,2},{1,5},{2,0},{3,7},{4,6},{5,1},{6,4},{7,3},{8,10},{9,13},{10,... | collective-permute-start | bytes 1572872 | tf_op jit(solution)/shard_map/ppermute | solution.py:239
  238.3 11.0 %collective-permute-start.66 = (bf16[1,8,128,128]{3,2,1,0:T(8,128)(2,1)S(1)}, bf16[1,8,128,128]{3,2,1,0:T(8,128)(2,1)S(1)}, u32[]{:S(2)}, u32[]{:S(2)}) collective-permute-start(bf16[1,8,128,128]{3,2,1,0:T(8,128)(2,1)S(1)} %add.33), channel_id=1, source_target_pairs={{0,4},{1,3},{2,6},{3,1},{4,0},{5,7},{6,2},{7,5},{8,12},{9,11},{10,... | collective-permute-start | bytes 786440 | tf_op jit(solution)/shard_map/ppermute | solution.py:239
  249.4 8.2 %collective-permute-start.67 = (bf16[8,32,128]{2,1,0:T(8,128)(2,1)S(1)}, bf16[8,32,128]{2,1,0:T(8,128)(2,1)S(1)}, u32[]{:S(2)}, u32[]{:S(2)}) collective-permute-start(bf16[8,32,128]{2,1,0:T(8,128)(2,1)S(1)} %get-tuple-element.163), channel_id=1, source_target_pairs={{0,8},{8,0},{16,24},{24,16},{1,9},{9,1},{17,25},{25,17},{2,10},{10... | collective-permute-start | bytes 196616 | tf_op jit(solution)/shard_map/ppermute | solution.py:242
  249.5 10.2 %collective-permute-start.68 = (bf16[8,32,128]{2,1,0:T(8,128)(2,1)S(1)}, bf16[8,32,128]{2,1,0:T(8,128)(2,1)S(1)}, u32[]{:S(2)}, u32[]{:S(2)}) collective-permute-start(bf16[8,32,128]{2,1,0:T(8,128)(2,1)S(1)} %get-tuple-element.164), channel_id=1, source_target_pairs={{0,16},{8,24},{16,0},{24,8},{1,17},{9,25},{17,1},{25,9},{2,18},{10... | collective-permute-start | bytes 196616 | tf_op jit(solution)/shard_map/ppermute | solution.py:242
  255.2 9.6 %collective-permute-start.58 = (bf16[8,32,128]{2,1,0:T(8,128)(2,1)S(1)}, bf16[8,32,128]{2,1,0:T(8,128)(2,1)S(1)}, u32[]{:S(2)}, u32[]{:S(2)}) collective-permute-start(bf16[8,32,128]{2,1,0:T(8,128)(2,1)S(1)} %get-tuple-element.153), channel_id=1, source_target_pairs={{0,8},{8,0},{16,24},{24,16},{1,9},{9,1},{17,25},{25,17},{2,10},{10... | collective-permute-start | bytes 196616 | tf_op jit(solution)/shard_map/ppermute | solution.py:242
  255.3 11.6 %collective-permute-start.59 = (bf16[8,32,128]{2,1,0:T(8,128)(2,1)S(1)}, bf16[8,32,128]{2,1,0:T(8,128)(2,1)S(1)}, u32[]{:S(2)}, u32[]{:S(2)}) collective-permute-start(bf16[8,32,128]{2,1,0:T(8,128)(2,1)S(1)} %get-tuple-element.154), channel_id=1, source_target_pairs={{0,16},{8,24},{16,0},{24,8},{1,17},{9,25},{17,1},{25,9},{2,18},{10... | collective-permute-start | bytes 196616 | tf_op jit(solution)/shard_map/ppermute | solution.py:242
  257.6 9.2 %collective-permute-start.60 = (bf16[8,32,128]{2,1,0:T(8,128)(2,1)S(1)}, bf16[8,32,128]{2,1,0:T(8,128)(2,1)S(1)}, u32[]{:S(2)}, u32[]{:S(2)}) collective-permute-start(bf16[8,32,128]{2,1,0:T(8,128)(2,1)S(1)} %get-tuple-element.155), channel_id=1, source_target_pairs={{0,24},{8,16},{16,8},{24,0},{1,25},{9,17},{17,9},{25,1},{2,26},{10... | collective-permute-start | bytes 196616 | tf_op jit(solution)/shard_map/ppermute | solution.py:242
  262.4 9.6 %collective-permute-start.70 = (bf16[8,32,128]{2,1,0:T(8,128)(2,1)S(1)}, bf16[8,32,128]{2,1,0:T(8,128)(2,1)S(1)}, u32[]{:S(2)}, u32[]{:S(2)}) collective-permute-start(bf16[8,32,128]{2,1,0:T(8,128)(2,1)S(1)} %get-tuple-element.167), channel_id=1, source_target_pairs={{0,8},{8,0},{16,24},{24,16},{1,9},{9,1},{17,25},{25,17},{2,10},{10... | collective-permute-start | bytes 196616 | tf_op jit(solution)/shard_map/ppermute | solution.py:242
  262.5 13.2 %collective-permute-start.71 = (bf16[8,32,128]{2,1,0:T(8,128)(2,1)S(1)}, bf16[8,32,128]{2,1,0:T(8,128)(2,1)S(1)}, u32[]{:S(2)}, u32[]{:S(2)}) collective-permute-start(bf16[8,32,128]{2,1,0:T(8,128)(2,1)S(1)} %get-tuple-element.168), channel_id=1, source_target_pairs={{0,16},{8,24},{16,0},{24,8},{1,17},{9,25},{17,1},{25,9},{2,18},{10... | collective-permute-start | bytes 196616 | tf_op jit(solution)/shard_map/ppermute | solution.py:242
  264.8 10.8 %collective-permute-start.72 = (bf16[8,32,128]{2,1,0:T(8,128)(2,1)S(1)}, bf16[8,32,128]{2,1,0:T(8,128)(2,1)S(1)}, u32[]{:S(2)}, u32[]{:S(2)}) collective-permute-start(bf16[8,32,128]{2,1,0:T(8,128)(2,1)S(1)} %get-tuple-element.169), channel_id=1, source_target_pairs={{0,24},{8,16},{16,8},{24,0},{1,25},{9,17},{17,9},{25,1},{2,26},{10... | collective-permute-start | bytes 196616 | tf_op jit(solution)/shard_map/ppermute | solution.py:242
  (56 other events, 389.3 us)

commit v2 on v0

v2 whole, which is shorter than its diff:
```python
import functools
import math

import jax
import jax.numpy as jnp
import ml_dtypes
import numpy as np
from jax import lax
from jax.experimental import pallas as pl
from jax.experimental.pallas import tpu as pltpu
from jax.sharding import PartitionSpec as P

NT = 512
ITERS = 2
KEPT = 192
PIECES = 2
TILE = 16
MIB = 1 << 20
BF16, F32 = jnp.bfloat16, jnp.float32


def window_tables(nfreq, pieces, groups):
    freqs = np.arange(1, nfreq + 1)
    times = np.arange(KEPT)
    phase = ((freqs[:, None] * times[None, :]) % NT).astype(np.float32) * np.float32(2.0 * math.pi / NT)
    parts = np.stack([np.cos(phase), -np.sin(phase)])
    inverse = (parts * np.float32(2.0 / NT)).astype(ml_dtypes.bfloat16)
    forward = parts.astype(ml_dtypes.bfloat16).astype(np.float32) * np.where(times == 0, 1.0, 2.0)
    forward = forward.astype(ml_dtypes.bfloat16)

    def rows(table):
        table = table.reshape(2, groups, pieces, nfreq // groups // pieces, KEPT)
        return table.transpose(2, 0, 1, 3, 4).reshape(pieces, 2 * nfreq // pieces, KEPT)

    return [np.ascontiguousarray(t.T) for t in rows(inverse)], [np.ascontiguousarray(t) for t in rows(forward)]


def lane_index(shape):
    return lax.broadcasted_iota(jnp.int32, shape, len(shape) - 1)


def pack_kernel(pieces, f_dev, rows, dw_ref, arrival_ref, *refs):
    fp = f_dev // pieces
    tables, out_refs = refs[: 2 * pieces], refs[2 * pieces :]
    for piece in range(pieces):
        for b in range(fp):
            value = dw_ref[pl.ds(piece * fp + b, rows, stride=f_dev), :]
            out_refs[piece][b] = value
            out_refs[pieces + piece][b] = value.astype(BF16)
    out_refs[2 * pieces][...] = jnp.concatenate([arrival_ref[...]] * 2, axis=1)
    for table, out in zip(tables, out_refs[2 * pieces + 1 :]):
        out[...] = table[...]


def unpack_kernel(pieces, f_dev, rows, has_wave, *refs):
    fp = f_dev // pieces
    out_ref = refs[-1]
    for piece in range(pieces):
        for b in range(fp):
            value = refs[piece][b].astype(F32)
            place = pl.ds(piece * fp + b, rows, stride=f_dev)
            if has_wave:
                value = value + refs[pieces][place, :]
            out_ref[place, :] = value


def assemble_kernel(n_f, has_wave, where_ref, *refs):
    blocks, out_ref = refs[:n_f], refs[-1]
    rows = blocks[0].shape[1]
    for k in range(n_f):
        place = pl.ds(pl.multiple_of((where_ref[0] ^ k) * rows, rows), rows)
        value = blocks[k][...]
        if has_wave:
            value = (refs[n_f][:, place, :] + value.astype(F32)).astype(BF16)
        out_ref[:, place, :] = value


def half_kernel(first, core_ref, whole_ref, half_ref, sem):
    place = pl.ds(first, half_ref.shape[1])
    copy = pltpu.make_async_copy(whole_ref.at[:, place, :, core_ref[0]], half_ref, sem)
    copy.start()
    copy.wait()


def terms_kernel(n_chip, sign, order_ref, own_ref, other_ref, v_ref, w_ref, *refs):
    keep_ref, send_ref = refs[-2:]
    half = n_chip // 2
    lanes = lane_index(v_ref.shape[1:])
    for b in range(v_ref.shape[0]):
        rows = []
        for ref in (v_ref, w_ref):
            value = ref[b].astype(F32)
            turned = pltpu.roll(value, 64, 1)
            rows += [value, jnp.where((lanes < 64) == (sign > 0), -turned, turned)]
        weights = jnp.concatenate(rows, axis=0).astype(BF16)
        for pos in range(n_chip):
            at = order_ref[pos]
            left = [ref[p, b, at] for ref in (own_ref, other_ref) for p in range(2)]
            total = jnp.dot(jnp.concatenate(left, axis=1), weights, preferred_element_type=F32).astype(BF16)
            if pos < half:
                keep_ref[pos, b] = total
            else:
                send_ref[pos - half, b] = total


def add_kernel(n_in, *refs):
    out_ref = refs[-1]
    half = out_ref.shape[0]
    total = refs[0][half : 2 * half].astype(F32)
    for ref in refs[1:n_in]:
        total = total + ref[half : 2 * half].astype(F32)
    out_ref[...] = total.astype(BF16)


def split_kernel(n_in, n_f, where_ref, *refs):
    outs = refs[-n_f:]
    rows = outs[0].shape[1]
    for k in range(n_f):
        place = pl.ds(pl.multiple_of((where_ref[0] ^ k) * rows, rows), rows)
        total = refs[0][0, :, place, :].astype(F32)
        for ref in refs[1:n_in]:
            total = total + ref[0, :, place, :].astype(F32)
        outs[k][...] = total.astype(BF16)


def gather_rows(where_ref, blocks, gather):
    fp, rows, _ = blocks[0].shape
    depth = len(blocks) * fp
    for k, block in enumerate(blocks):
        base = (where_ref[0] ^ k) * fp
        for b in range(fp):
            gather[pl.ds(base + b, rows, stride=depth), :] = block[b].astype(F32)


def signal_of(inv_ref, gather, first, tile):
    depth = inv_ref.shape[1] // 2
    real = lane_index((depth, 128)) < 64
    columns = []
    for r in range(first, first + tile):
        value = gather[pl.ds(r * depth, depth), :]
        columns.append(jnp.concatenate([jnp.where(real, value, 0.0), jnp.where(real, 0.0, value)], axis=0).astype(BF16))
    return jnp.dot(inv_ref[...], jnp.concatenate(columns, axis=1), preferred_element_type=F32)


def scatter_back(fwd_ref, kept, scatter, first, tile):
    depth = fwd_ref.shape[0] // 2
    real = lane_index((depth, 128)) < 64
    back = jnp.dot(fwd_ref[...], kept, preferred_element_type=F32)
    for i in range(tile):
        columns = back[:, i * 128 : (i + 1) * 128]
        scatter[pl.ds((first + i) * depth, depth), :] = jnp.where(real, columns[:depth], columns[depth:])


def scatter_rows(where_ref, scatter, outs):
    fp, rows, _ = outs[0].shape
    depth = len(outs) * fp
    for k, out in enumerate(outs):
        base = (where_ref[0] ^ k) * fp
        for b in range(fp):
            out[b] = scatter[pl.ds(base + b, rows, stride=depth), :].astype(BF16)


def signal_kernel(n_f, tile, where_ref, inv_ref, *refs):
    blocks, (signal_ref, gather) = refs[:n_f], refs[-2:]
    gather_rows(where_ref, blocks, gather)
    for first in range(0, blocks[0].shape[1], tile):
        signal_ref[:, first * 128 : (first + tile) * 128] = signal_of(inv_ref, gather, first, tile)


def window_kernel(n_f, n_signal, tile, where_ref, limit_ref, inv_ref, fwd_ref, *refs):
    blocks, signals = refs[:n_f], refs[n_f : n_f + n_signal]
    kept_ref, outs, (gather, scatter) = refs[-n_f - 3], refs[-n_f - 2 : -2], refs[-2:]
    times = lax.broadcasted_iota(jnp.int32, (KEPT, 128), 0)
    gather_rows(where_ref, blocks, gather)
    for first in range(0, blocks[0].shape[1], tile):
        signal = signal_of(inv_ref, gather, first, tile)
        for ref in signals:
            signal = signal + ref[:, first * 128 : (first + tile) * 128]
        kept = []
        for i in range(tile):
            limit = limit_ref[pl.ds(first + i, 1), :]
            kept.append(jnp.where(times < limit, signal[:, i * 128 : (i + 1) * 128], 0.0).astype(BF16))
        kept = jnp.concatenate(kept, axis=1)
        kept_ref[:, first * 128 : (first + tile) * 128] = kept
        scatter_back(fwd_ref, kept, scatter, first, tile)
    scatter_rows(where_ref, scatter, outs)


def back_kernel(n_f, tile, where_ref, fwd_ref, kept_ref, *refs):
    outs, scatter = refs[-n_f - 1 : -1], refs[-1]
    for first in range(0, outs[0].shape[1], tile):
        scatter_back(fwd_ref, kept_ref[:, first * 128 : (first + tile) * 128], scatter, first, tile)
    scatter_rows(where_ref, scatter, outs)


def vmem():
    return pl.BlockSpec(memory_space=pltpu.VMEM)


def smem():
    return pl.BlockSpec(memory_space=pltpu.SMEM)


def anywhere():
    return pl.BlockSpec(memory_space=pl.ANY)


def bf16(*shape):
    return jax.ShapeDtypeStruct(shape, BF16)


def call(kernel, name, outs, scalars, values, after=(), scratch=(), mib=12, weight=2e10):
    return pl.pallas_call(
        kernel,
        out_shape=outs,
        in_specs=[smem()] * len(scalars) + [vmem()] * len(values) + [anywhere()] * len(after),
        out_specs=[vmem()] * len(outs),
        scratch_shapes=list(scratch),
        compiler_params=pltpu.CompilerParams(vmem_limit_bytes=mib * MIB),
        cost_estimate=pl.CostEstimate(flops=int(weight), bytes_accessed=MIB, transcendentals=0),
        name=name,
    )(*scalars, *values, *after)


class Plan:
    def __init__(self, reflection, direct_wave, first_arrival):
        self.n_f, self.n_s = lax.axis_size("freq"), lax.axis_size("src")
        self.q, self.f_dev, _ = direct_wave.shape
        self.pieces = PIECES
        self.fp = self.f_dev // self.pieces
        self.own_rows = self.q // self.n_f
        self.tile = min(TILE, self.own_rows)
        self.n_chip = self.n_s // 2
        self.bits = self.n_chip.bit_length() - 1
        z, s = lax.axis_index("freq"), lax.axis_index("src")
        chip, core = s // 2, s % 2
        self.where = z.reshape(1).astype(jnp.int32)
        orders = np.zeros((2, self.n_chip), np.int32)
        for c in range(2):
            for pos in range(self.n_chip):
                for stage in range(self.bits):
                    if pos >> (self.bits - 1 - stage) & 1:
                        orders[c, pos] ^= self.mask(stage, c)
        self.order = (chip ^ jnp.asarray(orders)[core]).astype(jnp.int32)
        self.whole = (self.fp, self.q, 128)
        reflection = reflection.reshape(2, self.f_dev, self.n_chip, 2, self.q, self.q)
        self.other = [self.to_core(self.half(reflection, 1 - core, i)) for i in range(self.pieces)]
        self.own = [self.half(reflection, core, i) for i in range(self.pieces)]
        self.pack(direct_wave, first_arrival)

    def mask(self, stage, core):
        return 1 << ((stage + core) % self.bits)

    def to_core(self, value):
        return lax.ppermute(value, "src", [(s, s ^ 1) for s in range(self.n_s)])

    def to_chip(self, value, stage):
        pairs = [(s, s ^ (self.mask(stage, s % 2) << 1)) for s in range(self.n_s)]
        return lax.ppermute(value, "src", pairs)

    def exchange(self, blocks):
        pairs = {k: [(z, z ^ k) for z in range(self.n_f)] for k in range(self.n_f)}
        moved = {k: lax.ppermute(blocks[k], "freq", pairs[k]) for k in range(self.n_f - 1, 0, -1)}
        return [blocks[0]] + [moved[k] for k in range(1, self.n_f)]

    def half(self, reflection, core, piece):
        return pl.pallas_call(
            functools.partial(half_kernel, piece * self.fp),
            out_shape=bf16(2, self.fp, self.n_chip, self.q, self.q),
            in_specs=[smem(), pl.BlockSpec(memory_space=pltpu.HBM)],
            out_specs=vmem(),
            scratch_shapes=[pltpu.SemaphoreType.DMA],
            compiler_params=pltpu.CompilerParams(vmem_limit_bytes=58 * MIB),
            name="half",
        )(core.reshape(1), reflection)

    def pack(self, direct_wave, first_arrival):
        n = self.pieces
        inverse, forward = window_tables(self.n_f * self.f_dev, n, self.n_f)
        tables = [jnp.asarray(t) for t in inverse + forward]
        limit = jax.ShapeDtypeStruct((self.own_rows, 128), jnp.int32)
        outs = [jax.ShapeDtypeStruct(self.whole, F32)] * n + [bf16(*self.whole)] * n + [limit]
        out = call(
            functools.partial(pack_kernel, n, self.f_dev, self.q),
            "pack",
            outs + [bf16(*t.shape) for t in tables],
            [],
            [direct_wave.reshape(self.q * self.f_dev, 128), first_arrival, *tables],
        )
        self.waves, self.start, self.limit = out[:n], out[n : 2 * n], out[2 * n]
        self.inverse, self.forward = out[2 * n + 1 : 3 * n + 1], out[3 * n + 1 :]

    def unpack(self, values, wave=None):
        waves = [] if wave is None else [wave.reshape(self.q * self.f_dev, 128)]
        out = call(
            functools.partial(unpack_kernel, self.pieces, self.f_dev, self.q, wave is not None),
            "unpack",
            [jax.ShapeDtypeStruct((self.q * self.f_dev, 128), F32)],
            [],
            [*values, *waves],
        )
        return out[0].reshape(self.q, self.f_dev, 128)

    def assemble(self, blocks, wave, after):
        waves = [] if wave is None else [wave]
        kernel = functools.partial(assemble_kernel, self.n_f, wave is not None)
        return call(kernel, "assemble", [bf16(*self.whole)], [self.where], [*blocks, *waves], after)[0]

    def terms(self, piece, vector, other_vector, sign, after):
        out = bf16(self.n_chip // 2, *self.whole)
        kernel = functools.partial(terms_kernel, self.n_chip, sign)
        values = [self.own[piece], self.other[piece], vector, other_vector]
        return call(kernel, "terms", [out, out], [self.order], values, after, mib=20)

    def add(self, values, after):
        out = bf16(values[-1].shape[0] // 2, *self.whole)
        return call(functools.partial(add_kernel, len(values)), "add", [out], [], values, after)[0]

    def split(self, values, after):
        outs = [bf16(self.fp, self.own_rows, 128)] * self.n_f
        kernel = functools.partial(split_kernel, len(values), self.n_f)
        return call(kernel, "split", outs, [self.where], values, after)

    def rows_scratch(self):
        return pltpu.VMEM((self.own_rows * self.n_f * self.fp, 128), F32)

    def signal(self, piece, blocks, after):
        out = jax.ShapeDtypeStruct((KEPT, self.own_rows * 128), F32)
        kernel = functools.partial(signal_kernel, self.n_f, self.tile)
        values = [self.inverse[piece], *blocks]
        return call(kernel, "signal", [out], [self.where], values, after, [self.rows_scratch()], 20)[0]

    def window(self, piece, back, blocks, signals, after):
        outs = [bf16(KEPT, self.own_rows * 128)] + [bf16(self.fp, self.own_rows, 128)] * self.n_f
        kernel = functools.partial(window_kernel, self.n_f, len(signals), self.tile)
        values = [self.limit, self.inverse[piece], self.forward[back], *blocks, *signals]
        scratch = [self.rows_scratch(), self.rows_scratch()]
        kept, *blocks = call(kernel, "window", outs, [self.where], values, after, scratch, 20)
        return kept, blocks

    def back(self, piece, kept, after):
        outs = [bf16(self.fp, self.own_rows, 128)] * self.n_f
        kernel = functools.partial(back_kernel, self.n_f, self.tile)
        values = [self.forward[piece], kept]
        return call(kernel, "back", outs, [self.where], values, after, [self.rows_scratch()], 20)

    def theta(self, vectors, sign, waves, after):
        pieces = range(self.pieces)
        held, addends = [], []
        for i in pieces:
            vector = vectors(i, after)
            keep, send = self.terms(i, vector, self.to_core(vector), sign, after if i == 0 else [send])
            held.append(vector)
            addends.append([keep, self.to_chip(send, 0)])
        after = [send]
        for stage in range(1, self.bits):
            for i in pieces:
                send = self.add(addends[i], after)
                addends[i].append(self.to_chip(send, stage))
                after = [send]
        blocks = []
        for i in pieces:
            sums = self.split(addends[i], after)
            blocks.append(self.exchange(sums))
            after = [sums[0]]
        signals = []
        for i in pieces[:-1]:
            signals.append(self.signal(i, blocks[i], after))
            after = [signals[-1]]
        kept, out = self.window(self.pieces - 1, 0, blocks[-1], signals, after)
        arrived, after = [self.exchange(out)], [out[0]]
        for i in pieces[1:]:
            out = self.back(i, kept, after)
            arrived.append(self.exchange(out))
            after = [out[0]]
        return held, lambda i, then: self.assemble(arrived[i], waves and waves[i], after if i == 0 else then), after


def local(reflection, direct_wave, first_arrival):
    plan = Plan(reflection, direct_wave, first_arrival)
    vectors, after = lambda i, then: plan.start[i], []
    for step in range(2 * ITERS):
        waves = plan.waves if step % 2 == 1 and step < 2 * ITERS - 1 else None
        held, vectors, after = plan.theta(vectors, 1 if step % 2 == 0 else -1, waves, after)
    return plan.unpack(held), plan.unpack([vectors(i, after) for i in range(plan.pieces)], direct_wave)


def solution(mesh):
    in_specs = (P(None, "freq", None, "src"), P("src", "freq", None), P(("src", "freq"), None))
    out_specs = (P("src", "freq", None), P("src", "freq", None))
    return jax.shard_map(local, mesh=mesh, in_specs=in_specs, out_specs=out_specs, check_vma=False)
```

time: 460 us -> 230 us (0.50)
  waiting for transfers between devices: 229 us -> 76.3 us
  blocking collectives: 106 us -> 0 us
  starting transfers between devices: 8.42 us -> 94.3 us
  Pallas kernels: 0 us -> 55.6 us
  local copies, waits for them, and re-layouts: 52.5 us -> 2.19 us
  matrix products: 44.6 us -> 0 us
  between operations: 14.1 us -> 1.34 us
    unnamed x8 -> x0, waiting for transfers between devices: 203 us -> none
    all_to_all x6 -> x0, blocking collectives: 106 us -> none  [the longest x3 56.7 us: to_owners(): lax.all_to_all(summed, 'freq', split_axis=0, concat_axis=1, tiled=True)]
    ppermute x0 -> x74, starting transfers between devices: none -> 94.3 us  [the longest x48 71.9 us: exchange(): lax.ppermute(blocks[k], 'freq', pairs[k])]
    ppermute x0 -> x74, waiting for transfers between devices: none -> 76.3 us  [the longest x16 46.5 us: to_chip(): return lax.ppermute(value, 'src', pairs)]
    pallas_call x0 -> x51, Pallas kernels: none -> 55.6 us  [the longest x47 43.6 us: call(): pl.pallas_call(kernel, out_shape=outs, in_specs=[smem()] * len(scalars) +...]
    dot_general x8 -> x0, matrix products: 44.6 us -> none  [the longest x4 32.7 us: to_owners(): jnp.einsum('pfrs,psfk->rfk', reflection, operand, preferred_element_type=...]
    unnamed x17 -> x36, local copies, waits for them, and re-layouts: 34.7 us -> 2.19 us
    all_to_all x2 -> x0, waiting for transfers between devices: 26.4 us -> none  [the longest x1 13.8 us: to_owners(): lax.all_to_all(summed, 'freq', split_axis=0, concat_axis=1, tiled=True)]
  transfers between devices with their start and end apart: 6 -> 74, of which waited for: 6 -> 35; matrix products, arithmetic and copies ran while one was open for 0% -> 0% of each run, Pallas kernels for 0% -> 18%
where the time goes in v2:
time: 230 us
  starting transfers between devices  94.3 us (41%)
  waiting for transfers between devices  76.3 us (33%)
  Pallas kernels  55.6 us (24%)
    ppermute x48, starting transfers between devices, exchange(): lax.ppermute(blocks[k], 'freq', pairs[k])  71.9 us
    ppermute x16, waiting for transfers between devices, to_chip(): return lax.ppermute(value, 'src', pairs)  46.5 us
    pallas_call x47, Pallas kernels, call(): pl.pallas_call(kernel, out_shape=outs, in_specs=[smem()] * len(scalars) +...  43.6 us
    ppermute x48, waiting for transfers between devices, exchange(): lax.ppermute(blocks[k], 'freq', pairs[k])  29.7 us
    ppermute x16, starting transfers between devices, to_chip(): return lax.ppermute(value, 'src', pairs)  20.8 us
    pallas_call x4, Pallas kernels, half(): pl.pallas_call(functools.partial(half_kernel, piece * self.fp), out_shape...  12 us
  transfers between devices with their start and end apart: 74, of which 35 were waited for; matrix products, arithmetic and copies ran while one was open for 0% of the time, Pallas kernels for 18%

profile of v2, /device:TPU:0, one launch (start us, length us, event | category | flops | bytes accessed | tf_op | source)
XLA Modules:
  0.0 229.8 jit_solution(8856973684456964655)
XLA Ops:
  0.7 3.1 %half.7 = bf16[2,8,4,128,128]{4,3,2,1,0:T(8,128)(2,1)} custom-call(s32[1]{0:T(128)} %bitcast.5.core_ref, bf16[2,16,4,2,128,128]{5,4,3,2,1,0:T(8,128)(2,1)} %bitcast.11), custom_call_target="tpu_custom_call" | custom-call | tf_op jit(solution)/shard_map/half/pallas_call | solution.py:267
  6.4 2.9 %half.5 = bf16[2,8,4,128,128]{4,3,2,1,0:T(8,128)(2,1)} custom-call(s32[1]{0:T(128)} %bitcast.5.core_ref, bf16[2,16,4,2,128,128]{5,4,3,2,1,0:T(8,128)(2,1)} %bitcast.12), custom_call_target="tpu_custom_call" | custom-call | tf_op jit(solution)/shard_map/half/pallas_call | solution.py:267
  9.9 3.0 %half.6.own_ref = bf16[2,8,4,128,128]{4,3,2,1,0:T(8,128)(2,1)} custom-call(s32[1]{0:T(128)} %bitcast.3.core_ref, bf16[2,16,4,2,128,128]{5,4,3,2,1,0:T(8,128)(2,1)} %bitcast.13), custom_call_target="tpu_custom_call" | custom-call | tf_op jit(solution)/shard_map/half/pallas_call | solution.py:267
  12.9 3.1 %half.4.own_ref = bf16[2,8,4,128,128]{4,3,2,1,0:T(8,128)(2,1)} custom-call(s32[1]{0:T(128)} %bitcast.3.core_ref, bf16[2,16,4,2,128,128]{5,4,3,2,1,0:T(8,128)(2,1)} %bitcast.14), custom_call_target="tpu_custom_call" | custom-call | tf_op jit(solution)/shard_map/half/pallas_call | solution.py:267
  16.1 3.1 %terms.8 = (bf16[2,8,128,128]{3,2,1,0:T(8,128)(2,1)S(1)}, bf16[2,8,128,128]{3,2,1,0:T(8,128)(2,1)S(1)}) custom-call(s32[4]{0:T(128)S(1)} %xor_bitcast_fusion.order_ref, bf16[2,8,4,128,128]{4,3,2,1,0:T(8,128)(2,1)S(1)} %copy-done.1, bf16[2,8,4,128,128]{4,3,2,1,0:T(8,128)(2,1)} %collective-permute-done.2.other_ref, ...), custom_call_target="tpu_custom_call" | custom-call | flops 20000000000 | bytes 1048576 | tf_op jit(solution)/shard_map/terms/pallas_call | solution.py:213
  19.2 3.0 %collective-permute-start.5 = (bf16[2,8,128,128]{3,2,1,0:T(8,128)(2,1)S(1)}, bf16[2,8,128,128]{3,2,1,0:T(8,128)(2,1)S(1)}, u32[]{:S(2)}, u32[]{:S(2)}) collective-permute-start(bf16[2,8,128,128]{3,2,1,0:T(8,128)(2,1)S(1)} %get-tuple-element.101.refs_0_), channel_id=1, source_target_pairs={{0,2},{1,5},{2,0},{3,7},{4,6},{5,1},{6,4},{7,3},{8,10},{9,13},{10,... | collective-permute-start | bytes 1572872 | tf_op jit(solution)/shard_map/ppermute | solution.py:259
  22.2 2.9 %terms.9 = (bf16[2,8,128,128]{3,2,1,0:T(8,128)(2,1)S(1)}, bf16[2,8,128,128]{3,2,1,0:T(8,128)(2,1)S(1)}) custom-call(s32[4]{0:T(128)S(1)} %xor_bitcast_fusion.order_ref, bf16[2,8,4,128,128]{4,3,2,1,0:T(8,128)(2,1)S(1)} %copy-done, bf16[2,8,4,128,128]{4,3,2,1,0:T(8,128)(2,1)} %collective-permute-done.other_ref, ...), custom_call_target="tpu_custom_call" | custom-call | flops 20000000000 | bytes 1048576 | tf_op jit(solution)/shard_map/terms/pallas_call | solution.py:213
  25.2 4.1 %collective-permute-done.5.refs_1_ = bf16[2,8,128,128]{3,2,1,0:T(8,128)(2,1)S(1)} collective-permute-done((bf16[2,8,128,128]{3,2,1,0:T(8,128)(2,1)S(1)}, bf16[2,8,128,128]{3,2,1,0:T(8,128)(2,1)S(1)}, u32[]{:S(2)}, u32[]{:S(2)}) %collective-permute-start.5) | collective-permute-done | bytes 524320 | tf_op jit(solution)/shard_map/ppermute | solution.py:259
  31.5 6.2 %collective-permute-done.4.refs_1_ = bf16[2,8,128,128]{3,2,1,0:T(8,128)(2,1)S(1)} collective-permute-done((bf16[2,8,128,128]{3,2,1,0:T(8,128)(2,1)S(1)}, bf16[2,8,128,128]{3,2,1,0:T(8,128)(2,1)S(1)}, u32[]{:S(2)}, u32[]{:S(2)}) %collective-permute-start.4) | collective-permute-done | bytes 524320 | tf_op jit(solution)/shard_map/ppermute | solution.py:259
  41.7 2.6 %collective-permute-start.12 = (bf16[8,32,128]{2,1,0:T(8,128)(2,1)S(1)}, bf16[8,32,128]{2,1,0:T(8,128)(2,1)S(1)}, u32[]{:S(2)}, u32[]{:S(2)}) collective-permute-start(bf16[8,32,128]{2,1,0:T(8,128)(2,1)S(1)} %get-tuple-element.112), channel_id=1, source_target_pairs={{0,16},{8,24},{16,0},{24,8},{1,17},{9,25},{17,1},{25,9},{2,18},{10... | collective-permute-start | bytes 196616 | tf_op jit(solution)/shard_map/ppermute | solution.py:263
  46.5 2.6 %collective-permute-start.9 = (bf16[8,32,128]{2,1,0:T(8,128)(2,1)S(1)}, bf16[8,32,128]{2,1,0:T(8,128)(2,1)S(1)}, u32[]{:S(2)}, u32[]{:S(2)}) collective-permute-start(bf16[8,32,128]{2,1,0:T(8,128)(2,1)S(1)} %get-tuple-element.108), channel_id=1, source_target_pairs={{0,16},{8,24},{16,0},{24,8},{1,17},{9,25},{17,1},{25,9},{2,18},{10... | collective-permute-start | bytes 196616 | tf_op jit(solution)/shard_map/ppermute | solution.py:263
  59.0 2.6 %collective-permute-start.20 = (bf16[8,32,128]{2,1,0:T(8,128)(2,1)S(1)}, bf16[8,32,128]{2,1,0:T(8,128)(2,1)S(1)}, u32[]{:S(2)}, u32[]{:S(2)}) collective-permute-start(bf16[8,32,128]{2,1,0:T(8,128)(2,1)S(1)} %get-tuple-element.122), channel_id=1, source_target_pairs={{0,24},{8,16},{16,8},{24,0},{1,25},{9,17},{17,9},{25,1},{2,26},{10... | collective-permute-start | bytes 196616 | tf_op jit(solution)/shard_map/ppermute | solution.py:263
  64.2 2.6 %collective-permute-start.16 = (bf16[8,32,128]{2,1,0:T(8,128)(2,1)S(1)}, bf16[8,32,128]{2,1,0:T(8,128)(2,1)S(1)}, u32[]{:S(2)}, u32[]{:S(2)}) collective-permute-start(bf16[8,32,128]{2,1,0:T(8,128)(2,1)S(1)} %get-tuple-element.119), channel_id=1, source_target_pairs={{0,24},{8,16},{16,8},{24,0},{1,25},{9,17},{17,9},{25,1},{2,26},{10... | collective-permute-start | bytes 196616 | tf_op jit(solution)/shard_map/ppermute | solution.py:263
  70.4 2.9 %terms.10 = (bf16[2,8,128,128]{3,2,1,0:T(8,128)(2,1)S(1)}, bf16[2,8,128,128]{3,2,1,0:T(8,128)(2,1)S(1)}) custom-call(s32[4]{0:T(128)S(1)} %copy-done.3, bf16[2,8,4,128,128]{4,3,2,1,0:T(8,128)(2,1)S(1)} %copy-done.1, bf16[2,8,4,128,128]{4,3,2,1,0:T(8,128)(2,1)} %collective-permute-done.2.other_ref, bf16[8,128,128]{2,1,0:T(8,128)(2,1)S(1)} %assemble.9.v_ref, ...), custom_call_target="tpu_custom_call" | custom-call | flops 20000000000 | bytes 1048576 | tf_op jit(solution)/shard_map/terms/pallas_call | solution.py:213
  74.9 2.9 %terms.11 = (bf16[2,8,128,128]{3,2,1,0:T(8,128)(2,1)S(1)}, bf16[2,8,128,128]{3,2,1,0:T(8,128)(2,1)S(1)}) custom-call(s32[4]{0:T(128)S(1)} %copy-done.3, bf16[2,8,4,128,128]{4,3,2,1,0:T(8,128)(2,1)S(1)} %copy-done, bf16[2,8,4,128,128]{4,3,2,1,0:T(8,128)(2,1)} %collective-permute-done.other_ref, bf16[8,128,128]{2,1,0:T(8,128)(2,1)S(1)} %assemble.8.v_ref, ...), custom_call_target="tpu_custom_call" | custom-call | flops 20000000000 | bytes 1048576 | tf_op jit(solution)/shard_map/terms/pallas_call | solution.py:213
  78.4 4.1 %collective-permute-done.23.refs_1_ = bf16[2,8,128,128]{3,2,1,0:T(8,128)(2,1)S(1)} collective-permute-done((bf16[2,8,128,128]{3,2,1,0:T(8,128)(2,1)S(1)}, bf16[2,8,128,128]{3,2,1,0:T(8,128)(2,1)S(1)}, u32[]{:S(2)}, u32[]{:S(2)}) %collective-permute-start.23) | collective-permute-done | bytes 524320 | tf_op jit(solution)/shard_map/ppermute | solution.py:259
  83.9 7.1 %collective-permute-done.22.refs_1_ = bf16[2,8,128,128]{3,2,1,0:T(8,128)(2,1)S(1)} collective-permute-done((bf16[2,8,128,128]{3,2,1,0:T(8,128)(2,1)S(1)}, bf16[2,8,128,128]{3,2,1,0:T(8,128)(2,1)S(1)}, u32[]{:S(2)}, u32[]{:S(2)}) %collective-permute-start.22) | collective-permute-done | bytes 524320 | tf_op jit(solution)/shard_map/ppermute | solution.py:259
  93.1 2.9 %collective-permute-start.30 = (bf16[8,32,128]{2,1,0:T(8,128)(2,1)S(1)}, bf16[8,32,128]{2,1,0:T(8,128)(2,1)S(1)}, u32[]{:S(2)}, u32[]{:S(2)}) collective-permute-start(bf16[8,32,128]{2,1,0:T(8,128)(2,1)S(1)} %get-tuple-element.133), channel_id=1, source_target_pairs={{0,16},{8,24},{16,0},{24,8},{1,17},{9,25},{17,1},{25,9},{2,18},{10... | collective-permute-start | bytes 196616 | tf_op jit(solution)/shard_map/ppermute | solution.py:263
  97.7 3.1 %collective-permute-start.27 = (bf16[8,32,128]{2,1,0:T(8,128)(2,1)S(1)}, bf16[8,32,128]{2,1,0:T(8,128)(2,1)S(1)}, u32[]{:S(2)}, u32[]{:S(2)}) collective-permute-start(bf16[8,32,128]{2,1,0:T(8,128)(2,1)S(1)} %get-tuple-element.130), channel_id=1, source_target_pairs={{0,16},{8,24},{16,0},{24,8},{1,17},{9,25},{17,1},{25,9},{2,18},{10... | collective-permute-start | bytes 196616 | tf_op jit(solution)/shard_map/ppermute | solution.py:263
  110.8 2.5 %collective-permute-start.38 = (bf16[8,32,128]{2,1,0:T(8,128)(2,1)S(1)}, bf16[8,32,128]{2,1,0:T(8,128)(2,1)S(1)}, u32[]{:S(2)}, u32[]{:S(2)}) collective-permute-start(bf16[8,32,128]{2,1,0:T(8,128)(2,1)S(1)} %get-tuple-element.144), channel_id=1, source_target_pairs={{0,24},{8,16},{16,8},{24,0},{1,25},{9,17},{17,9},{25,1},{2,26},{10... | collective-permute-start | bytes 196616 | tf_op jit(solution)/shard_map/ppermute | solution.py:263
  116.0 2.5 %collective-permute-start.34 = (bf16[8,32,128]{2,1,0:T(8,128)(2,1)S(1)}, bf16[8,32,128]{2,1,0:T(8,128)(2,1)S(1)}, u32[]{:S(2)}, u32[]{:S(2)}) collective-permute-start(bf16[8,32,128]{2,1,0:T(8,128)(2,1)S(1)} %get-tuple-element.140), channel_id=1, source_target_pairs={{0,24},{8,16},{16,8},{24,0},{1,25},{9,17},{17,9},{25,1},{2,26},{10... | collective-permute-start | bytes 196616 | tf_op jit(solution)/shard_map/ppermute | solution.py:263
  122.8 2.9 %terms.12 = (bf16[2,8,128,128]{3,2,1,0:T(8,128)(2,1)S(1)}, bf16[2,8,128,128]{3,2,1,0:T(8,128)(2,1)S(1)}) custom-call(s32[4]{0:T(128)S(1)} %copy-done.4, bf16[2,8,4,128,128]{4,3,2,1,0:T(8,128)(2,1)S(1)} %copy-done.1, bf16[2,8,4,128,128]{4,3,2,1,0:T(8,128)(2,1)} %collective-permute-done.2.other_ref, bf16[8,128,128]{2,1,0:T(8,128)(2,1)S(1)} %assemble.11.v_ref, ...), custom_call_target="tpu_custom_call" | custom-call | flops 20000000000 | bytes 1048576 | tf_op jit(solution)/shard_map/terms/pallas_call | solution.py:213
  127.3 2.9 %terms.13 = (bf16[2,8,128,128]{3,2,1,0:T(8,128)(2,1)S(1)}, bf16[2,8,128,128]{3,2,1,0:T(8,128)(2,1)S(1)}) custom-call(s32[4]{0:T(128)S(1)} %copy-done.4, bf16[2,8,4,128,128]{4,3,2,1,0:T(8,128)(2,1)S(1)} %copy-done, bf16[2,8,4,128,128]{4,3,2,1,0:T(8,128)(2,1)} %collective-permute-done.other_ref, bf16[8,128,128]{2,1,0:T(8,128)(2,1)S(1)} %assemble.10.v_ref, ...), custom_call_target="tpu_custom_call" | custom-call | flops 20000000000 | bytes 1048576 | tf_op jit(solution)/shard_map/terms/pallas_call | solution.py:213
  130.8 4.1 %collective-permute-done.41.refs_1_ = bf16[2,8,128,128]{3,2,1,0:T(8,128)(2,1)S(1)} collective-permute-done((bf16[2,8,128,128]{3,2,1,0:T(8,128)(2,1)S(1)}, bf16[2,8,128,128]{3,2,1,0:T(8,128)(2,1)S(1)}, u32[]{:S(2)}, u32[]{:S(2)}) %collective-permute-start.41) | collective-permute-done | bytes 524320 | tf_op jit(solution)/shard_map/ppermute | solution.py:259
  136.2 7.3 %collective-permute-done.40.refs_1_ = bf16[2,8,128,128]{3,2,1,0:T(8,128)(2,1)S(1)} collective-permute-done((bf16[2,8,128,128]{3,2,1,0:T(8,128)(2,1)S(1)}, bf16[2,8,128,128]{3,2,1,0:T(8,128)(2,1)S(1)}, u32[]{:S(2)}, u32[]{:S(2)}) %collective-permute-start.40) | collective-permute-done | bytes 524320 | tf_op jit(solution)/shard_map/ppermute | solution.py:259
  145.6 2.7 %collective-permute-start.48 = (bf16[8,32,128]{2,1,0:T(8,128)(2,1)S(1)}, bf16[8,32,128]{2,1,0:T(8,128)(2,1)S(1)}, u32[]{:S(2)}, u32[]{:S(2)}) collective-permute-start(bf16[8,32,128]{2,1,0:T(8,128)(2,1)S(1)} %get-tuple-element.156), channel_id=1, source_target_pairs={{0,16},{8,24},{16,0},{24,8},{1,17},{9,25},{17,1},{25,9},{2,18},{10... | collective-permute-start | bytes 196616 | tf_op jit(solution)/shard_map/ppermute | solution.py:263
  164.0 2.4 %collective-permute-start.55 = (bf16[8,32,128]{2,1,0:T(8,128)(2,1)S(1)}, bf16[8,32,128]{2,1,0:T(8,128)(2,1)S(1)}, u32[]{:S(2)}, u32[]{:S(2)}) collective-permute-start(bf16[8,32,128]{2,1,0:T(8,128)(2,1)S(1)} %get-tuple-element.166), channel_id=1, source_target_pairs={{0,24},{8,16},{16,8},{24,0},{1,25},{9,17},{17,9},{25,1},{2,26},{10... | collective-permute-start | bytes 196616 | tf_op jit(solution)/shard_map/ppermute | solution.py:263
  176.2 3.2 %terms.14 = (bf16[2,8,128,128]{3,2,1,0:T(8,128)(2,1)S(1)}, bf16[2,8,128,128]{3,2,1,0:T(8,128)(2,1)S(1)}) custom-call(s32[4]{0:T(128)S(1)} %copy-done.5, bf16[2,8,4,128,128]{4,3,2,1,0:T(8,128)(2,1)S(1)} %copy-done.1, bf16[2,8,4,128,128]{4,3,2,1,0:T(8,128)(2,1)} %collective-permute-done.2.other_ref, bf16[8,128,128]{2,1,0:T(8,128)(2,1)S(1)} %assemble.12.refs_0_.v_ref, ...), custom_call_target="tpu_custom_call" | custom-call | flops 20000000000 | bytes 1048576 | tf_op jit(solution)/shard_map/terms/pallas_call | solution.py:213
  180.9 2.9 %terms.15 = (bf16[2,8,128,128]{3,2,1,0:T(8,128)(2,1)S(1)}, bf16[2,8,128,128]{3,2,1,0:T(8,128)(2,1)S(1)}) custom-call(s32[4]{0:T(128)S(1)} %copy-done.5, bf16[2,8,4,128,128]{4,3,2,1,0:T(8,128)(2,1)S(1)} %copy-done, bf16[2,8,4,128,128]{4,3,2,1,0:T(8,128)(2,1)} %collective-permute-done.other_ref, bf16[8,128,128]{2,1,0:T(8,128)(2,1)S(1)} %assemble.13.refs_1_.v_ref, ...), custom_call_target="tpu_custom_call" | custom-call | flops 20000000000 | bytes 1048576 | tf_op jit(solution)/shard_map/terms/pallas_call | solution.py:213
  184.4 4.1 %collective-permute-done.59.refs_1_ = bf16[2,8,128,128]{3,2,1,0:T(8,128)(2,1)S(1)} collective-permute-done((bf16[2,8,128,128]{3,2,1,0:T(8,128)(2,1)S(1)}, bf16[2,8,128,128]{3,2,1,0:T(8,128)(2,1)S(1)}, u32[]{:S(2)}, u32[]{:S(2)}) %collective-permute-start.59) | collective-permute-done | bytes 524320 | tf_op jit(solution)/shard_map/ppermute | solution.py:259
  189.8 7.2 %collective-permute-done.58.refs_1_ = bf16[2,8,128,128]{3,2,1,0:T(8,128)(2,1)S(1)} collective-permute-done((bf16[2,8,128,128]{3,2,1,0:T(8,128)(2,1)S(1)}, bf16[2,8,128,128]{3,2,1,0:T(8,128)(2,1)S(1)}, u32[]{:S(2)}, u32[]{:S(2)}) %collective-permute-start.58) | collective-permute-done | bytes 524320 | tf_op jit(solution)/shard_map/ppermute | solution.py:259
  203.7 2.9 %collective-permute-start.63 = (bf16[8,32,128]{2,1,0:T(8,128)(2,1)S(1)}, bf16[8,32,128]{2,1,0:T(8,128)(2,1)S(1)}, u32[]{:S(2)}, u32[]{:S(2)}) collective-permute-start(bf16[8,32,128]{2,1,0:T(8,128)(2,1)S(1)} %get-tuple-element.174), channel_id=1, source_target_pairs={{0,16},{8,24},{16,0},{24,8},{1,17},{9,25},{17,1},{25,9},{2,18},{10... | collective-permute-start | bytes 196616 | tf_op jit(solution)/shard_map/ppermute | solution.py:263
  (204 shorter events, 115.7 us)
Async XLA Ops:
  3.8 12.3 %collective-permute-start.2 = (bf16[2,8,4,128,128]{4,3,2,1,0:T(8,128)(2,1)}, bf16[2,8,4,128,128]{4,3,2,1,0:T(8,128)(2,1)}, u32[]{:S(2)}, u32[]{:S(2)}) collective-permute-start(bf16[2,8,4,128,128]{4,3,2,1,0:T(8,128)(2,1)} %half.7), channel_id=1, source_target_pairs={{0,1},{1,0},{2,3},{3,2},{4,5},{5,4},{6,7},{7,6},{8,9},{9,8},{10,11... | collective-permute-start | bytes 6291464 | tf_op jit(solution)/shard_map/ppermute | solution.py:255
  6.4 9.7 %collective-permute-start.3 = (bf16[8,128,128]{2,1,0:T(8,128)(2,1)S(1)}, bf16[8,128,128]{2,1,0:T(8,128)(2,1)S(1)}, u32[]{:S(2)}, u32[]{:S(2)}) collective-permute-start(bf16[8,128,128]{2,1,0:T(8,128)(2,1)S(1)} %get-tuple-element.100.v_ref), channel_id=1, source_target_pairs={{0,1},{1,0},{2,3},{3,2},{4,5},{5,4},{6,7},{7,6},{8,9},{9,8},{10,11... | collective-permute-start | bytes 786440 | tf_op jit(solution)/shard_map/ppermute | solution.py:255
  9.3 12.8 %collective-permute-start = (bf16[2,8,4,128,128]{4,3,2,1,0:T(8,128)(2,1)}, bf16[2,8,4,128,128]{4,3,2,1,0:T(8,128)(2,1)}, u32[]{:S(2)}, u32[]{:S(2)}) collective-permute-start(bf16[2,8,4,128,128]{4,3,2,1,0:T(8,128)(2,1)} %half.5), channel_id=1, source_target_pairs={{0,1},{1,0},{2,3},{3,2},{4,5},{5,4},{6,7},{7,6},{8,9},{9,8},{10,11... | collective-permute-start | bytes 6291464 | tf_op jit(solution)/shard_map/ppermute | solution.py:255
  9.9 12.3 %collective-permute-start.1 = (bf16[8,128,128]{2,1,0:T(8,128)(2,1)S(1)}, bf16[8,128,128]{2,1,0:T(8,128)(2,1)S(1)}, u32[]{:S(2)}, u32[]{:S(2)}) collective-permute-start(bf16[8,128,128]{2,1,0:T(8,128)(2,1)S(1)} %get-tuple-element.99.v_ref), channel_id=1, source_target_pairs={{0,1},{1,0},{2,3},{3,2},{4,5},{5,4},{6,7},{7,6},{8,9},{9,8},{10,11... | collective-permute-start | bytes 786440 | tf_op jit(solution)/shard_map/ppermute | solution.py:255
  19.2 10.1 %collective-permute-start.5 = (bf16[2,8,128,128]{3,2,1,0:T(8,128)(2,1)S(1)}, bf16[2,8,128,128]{3,2,1,0:T(8,128)(2,1)S(1)}, u32[]{:S(2)}, u32[]{:S(2)}) collective-permute-start(bf16[2,8,128,128]{3,2,1,0:T(8,128)(2,1)S(1)} %get-tuple-element.101.refs_0_), channel_id=1, source_target_pairs={{0,2},{1,5},{2,0},{3,7},{4,6},{5,1},{6,4},{7,3},{8,10},{9,13},{10,... | collective-permute-start | bytes 1572872 | tf_op jit(solution)/shard_map/ppermute | solution.py:259
  25.1 12.6 %collective-permute-start.4 = (bf16[2,8,128,128]{3,2,1,0:T(8,128)(2,1)S(1)}, bf16[2,8,128,128]{3,2,1,0:T(8,128)(2,1)S(1)}, u32[]{:S(2)}, u32[]{:S(2)}) collective-permute-start(bf16[2,8,128,128]{3,2,1,0:T(8,128)(2,1)S(1)} %get-tuple-element.103.refs_2_), channel_id=1, source_target_pairs={{0,2},{1,5},{2,0},{3,7},{4,6},{5,1},{6,4},{7,3},{8,10},{9,13},{10,... | collective-permute-start | bytes 1572872 | tf_op jit(solution)/shard_map/ppermute | solution.py:259
  29.4 10.5 %collective-permute-start.7 = (bf16[1,8,128,128]{3,2,1,0:T(8,128)(2,1)S(1)}, bf16[1,8,128,128]{3,2,1,0:T(8,128)(2,1)S(1)}, u32[]{:S(2)}, u32[]{:S(2)}) collective-permute-start(bf16[1,8,128,128]{3,2,1,0:T(8,128)(2,1)S(1)} %add.18.refs_2_), channel_id=1, source_target_pairs={{0,4},{1,3},{2,6},{3,1},{4,0},{5,7},{6,2},{7,5},{8,12},{9,11},{10,... | collective-permute-start | bytes 786440 | tf_op jit(solution)/shard_map/ppermute | solution.py:259
  40.0 9.1 %collective-permute-start.11 = (bf16[8,32,128]{2,1,0:T(8,128)(2,1)S(1)}, bf16[8,32,128]{2,1,0:T(8,128)(2,1)S(1)}, u32[]{:S(2)}, u32[]{:S(2)}) collective-permute-start(bf16[8,32,128]{2,1,0:T(8,128)(2,1)S(1)} %get-tuple-element.111), channel_id=1, source_target_pairs={{0,8},{8,0},{16,24},{24,16},{1,9},{9,1},{17,25},{25,17},{2,10},{10... | collective-permute-start | bytes 196616 | tf_op jit(solution)/shard_map/ppermute | solution.py:263
  41.7 8.2 %collective-permute-start.12 = (bf16[8,32,128]{2,1,0:T(8,128)(2,1)S(1)}, bf16[8,32,128]{2,1,0:T(8,128)(2,1)S(1)}, u32[]{:S(2)}, u32[]{:S(2)}) collective-permute-start(bf16[8,32,128]{2,1,0:T(8,128)(2,1)S(1)} %get-tuple-element.112), channel_id=1, source_target_pairs={{0,16},{8,24},{16,0},{24,8},{1,17},{9,25},{17,1},{25,9},{2,18},{10... | collective-permute-start | bytes 196616 | tf_op jit(solution)/shard_map/ppermute | solution.py:263
  57.2 9.5 %collective-permute-start.19 = (bf16[8,32,128]{2,1,0:T(8,128)(2,1)S(1)}, bf16[8,32,128]{2,1,0:T(8,128)(2,1)S(1)}, u32[]{:S(2)}, u32[]{:S(2)}) collective-permute-start(bf16[8,32,128]{2,1,0:T(8,128)(2,1)S(1)} %get-tuple-element.121), channel_id=1, source_target_pairs={{0,16},{8,24},{16,0},{24,8},{1,17},{9,25},{17,1},{25,9},{2,18},{10... | collective-permute-start | bytes 196616 | tf_op jit(solution)/shard_map/ppermute | solution.py:263
  59.0 7.8 %collective-permute-start.20 = (bf16[8,32,128]{2,1,0:T(8,128)(2,1)S(1)}, bf16[8,32,128]{2,1,0:T(8,128)(2,1)S(1)}, u32[]{:S(2)}, u32[]{:S(2)}) collective-permute-start(bf16[8,32,128]{2,1,0:T(8,128)(2,1)S(1)} %get-tuple-element.122), channel_id=1, source_target_pairs={{0,24},{8,16},{16,8},{24,0},{1,25},{9,17},{17,9},{25,1},{2,26},{10... | collective-permute-start | bytes 196616 | tf_op jit(solution)/shard_map/ppermute | solution.py:263
  73.3 9.2 %collective-permute-start.23 = (bf16[2,8,128,128]{3,2,1,0:T(8,128)(2,1)S(1)}, bf16[2,8,128,128]{3,2,1,0:T(8,128)(2,1)S(1)}, u32[]{:S(2)}, u32[]{:S(2)}) collective-permute-start(bf16[2,8,128,128]{3,2,1,0:T(8,128)(2,1)S(1)} %get-tuple-element.123.refs_0_), channel_id=1, source_target_pairs={{0,2},{1,5},{2,0},{3,7},{4,6},{5,1},{6,4},{7,3},{8,10},{9,13},{10,... | collective-permute-start | bytes 1572872 | tf_op jit(solution)/shard_map/ppermute | solution.py:259
  77.8 13.2 %collective-permute-start.22 = (bf16[2,8,128,128]{3,2,1,0:T(8,128)(2,1)S(1)}, bf16[2,8,128,128]{3,2,1,0:T(8,128)(2,1)S(1)}, u32[]{:S(2)}, u32[]{:S(2)}) collective-permute-start(bf16[2,8,128,128]{3,2,1,0:T(8,128)(2,1)S(1)} %get-tuple-element.125.refs_2_), channel_id=1, source_target_pairs={{0,2},{1,5},{2,0},{3,7},{4,6},{5,1},{6,4},{7,3},{8,10},{9,13},{10,... | collective-permute-start | bytes 1572872 | tf_op jit(solution)/shard_map/ppermute | solution.py:259
  82.6 9.7 %collective-permute-start.25 = (bf16[1,8,128,128]{3,2,1,0:T(8,128)(2,1)S(1)}, bf16[1,8,128,128]{3,2,1,0:T(8,128)(2,1)S(1)}, u32[]{:S(2)}, u32[]{:S(2)}) collective-permute-start(bf16[1,8,128,128]{3,2,1,0:T(8,128)(2,1)S(1)} %add.20.refs_2_), channel_id=1, source_target_pairs={{0,4},{1,3},{2,6},{3,1},{4,0},{5,7},{6,2},{7,5},{8,12},{9,11},{10,... | collective-permute-start | bytes 786440 | tf_op jit(solution)/shard_map/ppermute | solution.py:259
  92.4 8.4 %collective-permute-start.29 = (bf16[8,32,128]{2,1,0:T(8,128)(2,1)S(1)}, bf16[8,32,128]{2,1,0:T(8,128)(2,1)S(1)}, u32[]{:S(2)}, u32[]{:S(2)}) collective-permute-start(bf16[8,32,128]{2,1,0:T(8,128)(2,1)S(1)} %get-tuple-element.132), channel_id=1, source_target_pairs={{0,8},{8,0},{16,24},{24,16},{1,9},{9,1},{17,25},{25,17},{2,10},{10... | collective-permute-start | bytes 196616 | tf_op jit(solution)/shard_map/ppermute | solution.py:263
  93.1 8.9 %collective-permute-start.30 = (bf16[8,32,128]{2,1,0:T(8,128)(2,1)S(1)}, bf16[8,32,128]{2,1,0:T(8,128)(2,1)S(1)}, u32[]{:S(2)}, u32[]{:S(2)}) collective-permute-start(bf16[8,32,128]{2,1,0:T(8,128)(2,1)S(1)} %get-tuple-element.133), channel_id=1, source_target_pairs={{0,16},{8,24},{16,0},{24,8},{1,17},{9,25},{17,1},{25,9},{2,18},{10... | collective-permute-start | bytes 196616 | tf_op jit(solution)/shard_map/ppermute | solution.py:263
  108.9 9.5 %collective-permute-start.37 = (bf16[8,32,128]{2,1,0:T(8,128)(2,1)S(1)}, bf16[8,32,128]{2,1,0:T(8,128)(2,1)S(1)}, u32[]{:S(2)}, u32[]{:S(2)}) collective-permute-start(bf16[8,32,128]{2,1,0:T(8,128)(2,1)S(1)} %get-tuple-element.143), channel_id=1, source_target_pairs={{0,16},{8,24},{16,0},{24,8},{1,17},{9,25},{17,1},{25,9},{2,18},{10... | collective-permute-start | bytes 196616 | tf_op jit(solution)/shard_map/ppermute | solution.py:263
  110.8 7.7 %collective-permute-start.38 = (bf16[8,32,128]{2,1,0:T(8,128)(2,1)S(1)}, bf16[8,32,128]{2,1,0:T(8,128)(2,1)S(1)}, u32[]{:S(2)}, u32[]{:S(2)}) collective-permute-start(bf16[8,32,128]{2,1,0:T(8,128)(2,1)S(1)} %get-tuple-element.144), channel_id=1, source_target_pairs={{0,24},{8,16},{16,8},{24,0},{1,25},{9,17},{17,9},{25,1},{2,26},{10... | collective-permute-start | bytes 196616 | tf_op jit(solution)/shard_map/ppermute | solution.py:263
  125.7 9.2 %collective-permute-start.41 = (bf16[2,8,128,128]{3,2,1,0:T(8,128)(2,1)S(1)}, bf16[2,8,128,128]{3,2,1,0:T(8,128)(2,1)S(1)}, u32[]{:S(2)}, u32[]{:S(2)}) collective-permute-start(bf16[2,8,128,128]{3,2,1,0:T(8,128)(2,1)S(1)} %get-tuple-element.146.refs_0_), channel_id=1, source_target_pairs={{0,2},{1,5},{2,0},{3,7},{4,6},{5,1},{6,4},{7,3},{8,10},{9,13},{10,... | collective-permute-start | bytes 1572872 | tf_op jit(solution)/shard_map/ppermute | solution.py:259
  130.2 13.2 %collective-permute-start.40 = (bf16[2,8,128,128]{3,2,1,0:T(8,128)(2,1)S(1)}, bf16[2,8,128,128]{3,2,1,0:T(8,128)(2,1)S(1)}, u32[]{:S(2)}, u32[]{:S(2)}) collective-permute-start(bf16[2,8,128,128]{3,2,1,0:T(8,128)(2,1)S(1)} %get-tuple-element.148.refs_2_), channel_id=1, source_target_pairs={{0,2},{1,5},{2,0},{3,7},{4,6},{5,1},{6,4},{7,3},{8,10},{9,13},{10,... | collective-permute-start | bytes 1572872 | tf_op jit(solution)/shard_map/ppermute | solution.py:259
  135.0 9.6 %collective-permute-start.43 = (bf16[1,8,128,128]{3,2,1,0:T(8,128)(2,1)S(1)}, bf16[1,8,128,128]{3,2,1,0:T(8,128)(2,1)S(1)}, u32[]{:S(2)}, u32[]{:S(2)}) collective-permute-start(bf16[1,8,128,128]{3,2,1,0:T(8,128)(2,1)S(1)} %add.22.refs_2_), channel_id=1, source_target_pairs={{0,4},{1,3},{2,6},{3,1},{4,0},{5,7},{6,2},{7,5},{8,12},{9,11},{10,... | collective-permute-start | bytes 786440 | tf_op jit(solution)/shard_map/ppermute | solution.py:259
  144.8 8.4 %collective-permute-start.47 = (bf16[8,32,128]{2,1,0:T(8,128)(2,1)S(1)}, bf16[8,32,128]{2,1,0:T(8,128)(2,1)S(1)}, u32[]{:S(2)}, u32[]{:S(2)}) collective-permute-start(bf16[8,32,128]{2,1,0:T(8,128)(2,1)S(1)} %get-tuple-element.155), channel_id=1, source_target_pairs={{0,8},{8,0},{16,24},{24,16},{1,9},{9,1},{17,25},{25,17},{2,10},{10... | collective-permute-start | bytes 196616 | tf_op jit(solution)/shard_map/ppermute | solution.py:263
  145.6 8.9 %collective-permute-start.48 = (bf16[8,32,128]{2,1,0:T(8,128)(2,1)S(1)}, bf16[8,32,128]{2,1,0:T(8,128)(2,1)S(1)}, u32[]{:S(2)}, u32[]{:S(2)}) collective-permute-start(bf16[8,32,128]{2,1,0:T(8,128)(2,1)S(1)} %get-tuple-element.156), channel_id=1, source_target_pairs={{0,16},{8,24},{16,0},{24,8},{1,17},{9,25},{17,1},{25,9},{2,18},{10... | collective-permute-start | bytes 196616 | tf_op jit(solution)/shard_map/ppermute | solution.py:263
  162.1 8.8 %collective-permute-start.54 = (bf16[8,32,128]{2,1,0:T(8,128)(2,1)S(1)}, bf16[8,32,128]{2,1,0:T(8,128)(2,1)S(1)}, u32[]{:S(2)}, u32[]{:S(2)}) collective-permute-start(bf16[8,32,128]{2,1,0:T(8,128)(2,1)S(1)} %get-tuple-element.165), channel_id=1, source_target_pairs={{0,16},{8,24},{16,0},{24,8},{1,17},{9,25},{17,1},{25,9},{2,18},{10... | collective-permute-start | bytes 196616 | tf_op jit(solution)/shard_map/ppermute | solution.py:263
  170.9 10.0 %collective-permute-start.56 = (bf16[8,128,128]{2,1,0:T(8,128)(2,1)S(1)}, bf16[8,128,128]{2,1,0:T(8,128)(2,1)S(1)}, u32[]{:S(2)}, u32[]{:S(2)}) collective-permute-start(bf16[8,128,128]{2,1,0:T(8,128)(2,1)S(1)} %assemble.13.refs_1_.v_ref), channel_id=1, source_target_pairs={{0,1},{1,0},{2,3},{3,2},{4,5},{5,4},{6,7},{7,6},{8,9},{9,8},{10,11... | collective-permute-start | bytes 786440 | tf_op jit(solution)/shard_map/ppermute | solution.py:255
  179.3 9.2 %collective-permute-start.59 = (bf16[2,8,128,128]{3,2,1,0:T(8,128)(2,1)S(1)}, bf16[2,8,128,128]{3,2,1,0:T(8,128)(2,1)S(1)}, u32[]{:S(2)}, u32[]{:S(2)}) collective-permute-start(bf16[2,8,128,128]{3,2,1,0:T(8,128)(2,1)S(1)} %get-tuple-element.167.refs_0_), channel_id=1, source_target_pairs={{0,2},{1,5},{2,0},{3,7},{4,6},{5,1},{6,4},{7,3},{8,10},{9,13},{10,... | collective-permute-start | bytes 1572872 | tf_op jit(solution)/shard_map/ppermute | solution.py:259
  183.8 13.2 %collective-permute-start.58 = (bf16[2,8,128,128]{3,2,1,0:T(8,128)(2,1)S(1)}, bf16[2,8,128,128]{3,2,1,0:T(8,128)(2,1)S(1)}, u32[]{:S(2)}, u32[]{:S(2)}) collective-permute-start(bf16[2,8,128,128]{3,2,1,0:T(8,128)(2,1)S(1)} %get-tuple-element.169.refs_2_), channel_id=1, source_target_pairs={{0,2},{1,5},{2,0},{3,7},{4,6},{5,1},{6,4},{7,3},{8,10},{9,13},{10,... | collective-permute-start | bytes 1572872 | tf_op jit(solution)/shard_map/ppermute | solution.py:259
  188.7 9.6 %collective-permute-start.61 = (bf16[1,8,128,128]{3,2,1,0:T(8,128)(2,1)S(1)}, bf16[1,8,128,128]{3,2,1,0:T(8,128)(2,1)S(1)}, u32[]{:S(2)}, u32[]{:S(2)}) collective-permute-start(bf16[1,8,128,128]{3,2,1,0:T(8,128)(2,1)S(1)} %add.24.refs_2_), channel_id=1, source_target_pairs={{0,4},{1,3},{2,6},{3,1},{4,0},{5,7},{6,2},{7,5},{8,12},{9,11},{10,... | collective-permute-start | bytes 786440 | tf_op jit(solution)/shard_map/ppermute | solution.py:259
  198.3 8.3 %collective-permute-start.65 = (bf16[8,32,128]{2,1,0:T(8,128)(2,1)S(1)}, bf16[8,32,128]{2,1,0:T(8,128)(2,1)S(1)}, u32[]{:S(2)}, u32[]{:S(2)}) collective-permute-start(bf16[8,32,128]{2,1,0:T(8,128)(2,1)S(1)} %get-tuple-element.176), channel_id=1, source_target_pairs={{0,8},{8,0},{16,24},{24,16},{1,9},{9,1},{17,25},{25,17},{2,10},{10... | collective-permute-start | bytes 196616 | tf_op jit(solution)/shard_map/ppermute | solution.py:263
  199.3 8.7 %collective-permute-start.66 = (bf16[8,32,128]{2,1,0:T(8,128)(2,1)S(1)}, bf16[8,32,128]{2,1,0:T(8,128)(2,1)S(1)}, u32[]{:S(2)}, u32[]{:S(2)}) collective-permute-start(bf16[8,32,128]{2,1,0:T(8,128)(2,1)S(1)} %get-tuple-element.177), channel_id=1, source_target_pairs={{0,16},{8,24},{16,0},{24,8},{1,17},{9,25},{17,1},{25,9},{2,18},{10... | collective-permute-start | bytes 196616 | tf_op jit(solution)/shard_map/ppermute | solution.py:263
  203.7 7.7 %collective-permute-start.63 = (bf16[8,32,128]{2,1,0:T(8,128)(2,1)S(1)}, bf16[8,32,128]{2,1,0:T(8,128)(2,1)S(1)}, u32[]{:S(2)}, u32[]{:S(2)}) collective-permute-start(bf16[8,32,128]{2,1,0:T(8,128)(2,1)S(1)} %get-tuple-element.174), channel_id=1, source_target_pairs={{0,16},{8,24},{16,0},{24,8},{1,17},{9,25},{17,1},{25,9},{2,18},{10... | collective-permute-start | bytes 196616 | tf_op jit(solution)/shard_map/ppermute | solution.py:263
  215.4 9.0 %collective-permute-start.69 = (bf16[8,32,128]{2,1,0:T(8,128)(2,1)S(1)}, bf16[8,32,128]{2,1,0:T(8,128)(2,1)S(1)}, u32[]{:S(2)}, u32[]{:S(2)}) collective-permute-start(bf16[8,32,128]{2,1,0:T(8,128)(2,1)S(1)} %get-tuple-element.181), channel_id=1, source_target_pairs={{0,16},{8,24},{16,0},{24,8},{1,17},{9,25},{17,1},{25,9},{2,18},{10... | collective-permute-start | bytes 196616 | tf_op jit(solution)/shard_map/ppermute | solution.py:263
  (60 other events, 313.8 us)
